TPU v7x, 512 devices: a whole 4x4x16 slice. The times are simulated.
512 devices in a mesh: row: 32 (over y, x, core), col: 16 (over z).
Axes of the slice: x: 4, y: 4, z: 16, core: 2. Of those that a mesh axis runs over, the one named last changes fastest.
Arguments:
- features: bfloat16 [131072, 128], P('row'), may hold values from -4 to 4
- factor_prev: bfloat16 [131072, 2048], P('row', 'col'), may hold values from -0.125 to 0.125
- panel_index: int32 [1], replicated, may hold values from 0 to 511
Outputs:
- panel: float32 [131072, 256], P(('row', 'col'))
- log_det: float32 [1], replicated
All inputs are finite; a program needn't handle non-finite values.
Results may differ from a plain program's by a relative error of at most 0.0003.
Values may be sent and summed in bfloat16 or wider, within the bound.
No kernel may reach another device: no remote copies, remote signals or barrier semaphores. Data moves between devices by JAX's collectives and lax.ppermute only.
A program may use at most 64 MiB of HBM per device.

v0:
```python
import jax
import jax.numpy as jnp
from jax import lax
from jax.sharding import PartitionSpec as P

TILE = 256


NUGGET = 4.0
RANGE = 8.0


def spread(x, axis, root):
    mine = lax.axis_index(axis) == root
    return lax.psum(jnp.where(mine, x, jnp.zeros_like(x)), axis)


def kernel_block(row_feat, panel_feat, self_pair):
    row_wide = row_feat.astype(jnp.float32)
    panel_wide = panel_feat.astype(jnp.float32)
    row_square = jnp.sum(row_wide * row_wide, axis=1, keepdims=True)
    panel_square = jnp.sum(panel_wide * panel_wide, axis=1)[None, :]
    cross_term = jnp.dot(row_feat, panel_feat.T, preferred_element_type=jnp.float32)
    squared = jnp.maximum(row_square + panel_square - 2.0 * cross_term, 0.0)
    distance = jnp.where(self_pair, jnp.float32(0.0), jnp.sqrt(squared))
    return jnp.exp(-distance / RANGE) + jnp.where(self_pair, jnp.float32(NUGGET), jnp.float32(0.0))


def body(features, factor_prev, panel_index):
    row_count = lax.axis_size("row")
    col_count = lax.axis_size("col")
    rows_held = features.shape[0]
    my_rows = rows_held // col_count
    panel_tile = panel_index[0]
    owner_row = panel_tile % row_count
    local_tile = panel_tile // row_count
    own_feat = lax.dynamic_slice_in_dim(features, local_tile * TILE, TILE, 0)
    own_fac = lax.dynamic_slice_in_dim(factor_prev, local_tile * TILE, TILE, 0)
    panel_feat, panel_fac = (spread(own_feat, "row", owner_row), spread(own_fac, "row", owner_row))
    update = lax.psum_scatter(
        jnp.dot(factor_prev, panel_fac.T, preferred_element_type=jnp.float32),
        "col",
        scatter_dimension=0,
        tiled=True,
    )
    diagonal_part = jnp.dot(panel_fac, panel_fac.T, preferred_element_type=jnp.float32)
    diagonal_update = lax.psum(diagonal_part, "col")
    my_col = lax.axis_index("col")
    my_row = lax.axis_index("row")
    begin_mine = my_col * my_rows
    my_feat = lax.dynamic_slice_in_dim(features, begin_mine, my_rows, 0)
    local_index = begin_mine + jnp.arange(my_rows, dtype=jnp.int32)
    tile_of = local_index // TILE * row_count + my_row
    offset = local_index % TILE
    columns = jnp.arange(TILE, dtype=jnp.int32)
    self_pair = (tile_of == panel_tile)[:, None] & (offset[:, None] == columns[None, :])
    column_block = kernel_block(my_feat, panel_feat, self_pair) - update
    identity_mask = columns[:, None] == columns[None, :]
    diagonal = kernel_block(panel_feat, panel_feat, identity_mask) - diagonal_update
    diagonal_factor = jnp.linalg.cholesky(diagonal)
    identity = jnp.eye(TILE, dtype=jnp.float32)
    inverse = lax.linalg.triangular_solve(diagonal_factor, identity, left_side=True, lower=True)
    panel = jnp.dot(column_block, inverse.T, precision=lax.Precision.HIGHEST)
    panel = jnp.where((tile_of >= panel_tile)[:, None], panel, jnp.float32(0.0))
    log_det = 2.0 * jnp.sum(jnp.log(jnp.diagonal(diagonal_factor))) / TILE
    return (panel, jnp.reshape(log_det, (1,)))


def solution(mesh):
    in_specs = (P("row", None), P("row", "col"), P())
    out_specs = (P(("row", "col"), None), P())
    return jax.shard_map(body, mesh=mesh, in_specs=in_specs, out_specs=out_specs, check_vma=False)
```

profile of v0, /device:TPU:24, one launch (start us, length us, event | category | flops | bytes accessed | tf_op | source)
XLA Modules:
  0.0 374.7 jit_solution(8440229733805338883)
XLA Ops:
  7.2 0.0 all-reduce.7.cloned.1.call-start
  7.9 1.5 dynamic-slice_select_fusion
  9.4 0.0 all-reduce.7.cloned.1.call-update
  9.5 0.0 all-reduce.5.cloned.1.call-start
  9.5 137.2 %all-reduce.7.cloned.1.call-done = (bf16[256,128]{1,0:T(8,128)(2,1)}, bf16[256,128]{1,0:T(8,128)(2,1)}) async-done(((bf16[256,128]{1,0:T(8,128)(2,1)}, bf16[256,128]{1,0:T(8,128)(2,1)}), (bf16[256,128]{1,0:T(8,128)(2,1)}, bf16[256,128]{1,0:T(8,128)(2,1)})) %all-reduce.7.cloned.1.call-update) | async-done | bytes 131088 | tf_op jit(solution)/shard_map/psum | solution.py:15
  146.8 1.8 fusion.36
  148.6 0.0 all-reduce.5.cloned.1.call-update
  148.6 0.0 copy-start
  148.6 0.0 reduce-scatter.2.cloned.1.call-start
  148.6 3.9 %convolution_bitcast_fusion = f32[4096,256]{0,1:T(8,128)} fusion(bf16[256,128]{1,0:T(8,128)(2,1)} %get-tuple-element.30, bf16[4096,128]{1,0:T(8,128)(2,1)} %param.4), kind=kOutput, calls=%fused_computation.3 | convolution fusion | flops 268435456 | bytes 5308416 | tf_op jit(solution)/shard_map/dot_general | solution.py:41
  152.5 0.0 reduce-scatter.2.cloned.1.call-update
  152.6 1.0 multiply_reduce_fusion.1
  153.6 0.0 copy-done
  153.6 0.1 multiply_reduce_fusion
  153.8 131.0 %all-reduce.5.cloned.1.call-done = f32[256,256]{0,1:T(8,128)} async-done(((f32[256,256]{0,1:T(8,128)}), f32[256,256]{0,1:T(8,128)}) %all-reduce.5.cloned.1.call-update) | async-done | bytes 262160 | tf_op jit(solution)/shard_map/psum | solution.py:47
  284.8 1.3 fusion.15
  286.1 0.1 copy.16
  286.3 11.7 %cholesky.49 = f32[128,128]{1,0:T(8,128)S(1)} custom-call(f32[128,128]{1,0:T(8,128)S(1)} %cholesky.115), custom_call_target="Cholesky" | custom-call | tf_op jit(solution)/shard_map/jit(cholesky)/cholesky | solution.py:60
  298.0 0.1 copy.17
  298.1 9.8 %custom-call.14 = f32[1,128,128]{1,2,0:T(8,128)S(1)} custom-call(f32[1,128,128]{2,1,0:T(8,128)S(1)} %get-tuple-element.37), custom_call_target="InvertDiagBlocksLowerTriangular" | custom-call | tf_op jit(solution)/shard_map/jit(cholesky)/cholesky | solution.py:60
  307.9 0.2 fusion.28
  308.1 0.1 copy.18
  308.2 0.3 convolution_subtract_fusion.1
  308.5 11.7 %cholesky.103 = f32[128,128]{1,0:T(8,128)S(1)} custom-call(f32[128,128]{1,0:T(8,128)S(1)} %convolution_subtract_fusion.1), custom_call_target="Cholesky" | custom-call | tf_op jit(solution)/shard_map/jit(cholesky)/cholesky | solution.py:60
  320.2 0.1 copy.19
  320.4 0.6 compare_reduce_fusion.1
  321.0 0.6 compare_reduce_fusion
  323.0 0.1 triangular_solve.59
  323.1 4.4 %while.1 = (s32[]{:T(128)}, f32[256,256]{0,1:T(8,128)S(1)}, s32[2,2]{1,0:T(2,128)S(1)}, f32[2,128,128]{2,1,0:T(8,128)S(1)}, s32[]{:T(128)}) while((s32[]{:T(128)}, f32[256,256]{0,1:T(8,128)S(1)}, s32[2,2]{1,0:T(2,128)S(1)}, f32[2,128,128]{2,1,0:T(8,128)S(1)}, s32[]{:T(128)}) %tuple.31), condition=%wide.while_cond, body=%wide.while_body.sunk | while | flops 2 | bytes 393329 | solution.py:62
  323.3 0.6 fusion.50
  323.8 1.4 dynamic-slice.7
  325.2 0.1 copy.28
  325.4 0.6 fusion.50
  326.0 1.4 dynamic-slice.7
  327.3 0.1 copy.28
  327.5 19.7 %custom-call.15 = f32[2,128,128]{1,2,0:T(8,128)S(1)} custom-call(f32[2,128,128]{2,1,0:T(8,128)S(1)} %get-tuple-element.9), custom_call_target="InvertDiagBlocksLowerTriangular" | custom-call | tf_op jit(solution)/shard_map/triangular_solve | solution.py:62
  347.2 2.4 gather_fusion
  349.5 0.6 log_reduce_fusion
  350.8 0.3 fusion.24
  351.1 0.4 convolution_subtract_fusion
  351.5 0.3 fusion.27
  351.8 12.7 %reduce-scatter.2.cloned.1.call-done = f32[256,256]{0,1:T(8,128)} async-done(((f32[4096,256]{0,1:T(8,128)}), f32[256,256]{0,1:T(8,128)}) %reduce-scatter.2.cloned.1.call-update) | async-done | bytes 262160 | tf_op jit(solution)/shard_map/reduce_scatter | solution.py:40
  364.5 1.3 fusion.17
  365.8 0.4 convolution_select_fusion
  366.2 0.8 copy.22
  (18 shorter events, 0.3 us)
Async XLA Ops:
  7.2 139.6 %all-reduce.7.cloned.1.call-start = ((), (), s32[]{:S(2)}) async-start(), calls=%async_computation.3 | async-start | bytes 262144 | tf_op jit(solution)/shard_map/psum | solution.py:15
  9.5 275.3 %all-reduce.5.cloned.1.call-start = ((), (), s32[]{:S(2)}) async-start(), calls=%async_computation.2 | async-start | bytes 524288 | tf_op jit(solution)/shard_map/psum | solution.py:47
  148.6 5.1 %copy-start = (bf16[256,128]{1,0:T(8,128)(2,1)S(1)}, bf16[256,128]{1,0:T(8,128)(2,1)}, u32[]{:S(2)}) copy-start(bf16[256,128]{1,0:T(8,128)(2,1)} %get-tuple-element.31) | copy-start | bytes 196612
  148.6 215.9 %reduce-scatter.2.cloned.1.call-start = ((), (), s32[]{:S(2)}) async-start(), calls=%async_computation.1 | async-start | bytes 4456448 | tf_op jit(solution)/shard_map/reduce_scatter | solution.py:40
Sparse Core Ops, SparseCore 0:
  11.8 134.9 all-reduce.6
  149.7 135.0 all-reduce.4
  287.6 76.7 reduce-scatter.1
where the time goes:
time: 376 us; the launch traced here: 375 us
  waiting for transfers between devices  281 us (75%)
  other arithmetic  57.6 us (15%)
  between operations  17.7 us (5%)
  matrix products  10.1 us (3%)
  local copies, waits for them, and re-layouts  7.88 us (2%)
    psum x1, waiting for transfers between devices, spread(): return lax.psum(jnp.where(mine, x, jnp.zeros_like(x)), axis)  137 us
    psum x1, waiting for transfers between devices, body(): diagonal_update = lax.psum(diagonal_part, 'col')  131 us
    another operation x7, other arithmetic, body(): diagonal_factor = jnp.linalg.cholesky(diagonal)  34.6 us
    another operation x3, other arithmetic, body(): lax.linalg.triangular_solve(diagonal_factor, identity, left_side=True, lo...  19.7 us
    reduce_scatter x1, waiting for transfers between devices, body(): lax.psum_scatter(jnp.dot(factor_prev, panel_fac.T, preferred_element_type...  12.7 us
  transfers between devices with their start and end apart: 3, of which 3 were waited for; matrix products, arithmetic and copies ran while one was open for 19% of the time, Pallas kernels for 0%

commit v1 on v0

v1 whole, which is shorter than its diff:
```python
import jax
import jax.numpy as jnp
from jax import lax
from jax.sharding import PartitionSpec as P

TILE = 256
NUGGET = 4.0
RANGE = 8.0
CHUNKS = 8
PIECE = TILE // CHUNKS
FEAT_PIECE = 8
SLOT = PIECE + FEAT_PIECE


def kernel_block(row_feat, panel_feat, self_pair):
    row_wide = row_feat.astype(jnp.float32)
    panel_wide = panel_feat.astype(jnp.float32)
    row_square = jnp.sum(row_wide * row_wide, axis=1, keepdims=True)
    panel_square = jnp.sum(panel_wide * panel_wide, axis=1)[None, :]
    cross_term = jnp.dot(row_feat, panel_feat.T, preferred_element_type=jnp.float32)
    squared = jnp.maximum(row_square + panel_square - 2.0 * cross_term, 0.0)
    distance = jnp.where(self_pair, jnp.float32(0.0), jnp.sqrt(squared))
    return jnp.exp(-distance / RANGE) + jnp.where(self_pair, jnp.float32(NUGGET), jnp.float32(0.0))


def gather_panel(own_fac, own_feat, owner_row):
    width = own_fac.shape[1]
    col_count = lax.axis_size("col")
    my_col = lax.axis_index("col")
    fac_chunks = own_fac.reshape(CHUNKS, PIECE, width)
    feat_chunks = own_feat.reshape(CHUNKS, 4, FEAT_PIECE, width)
    feat_chunks = lax.dynamic_index_in_dim(feat_chunks, my_col % 4, 1, keepdims=False)
    slots = jnp.concatenate([fac_chunks, feat_chunks], axis=1)
    send = jnp.concatenate([slots] * 4, axis=0)
    got = lax.all_to_all(send, "row", 0, 0, tiled=True)
    slot = lax.dynamic_index_in_dim(got, owner_row, 0, keepdims=True)
    layers = lax.all_to_all(jnp.broadcast_to(slot, (col_count, SLOT, width)), "col", 0, 0, tiled=True)
    over_x = [[(y * 4 + x) * 2 + c for x in range(4)] for y in range(4) for c in range(2)]
    copies = jnp.broadcast_to(layers[None], (4, col_count, SLOT, width))
    mine = lax.all_to_all(copies, "row", 0, 0, tiled=True, axis_index_groups=over_x)
    other = lax.ppermute(mine, "row", [(i, i ^ 1) for i in range(32)])
    first = lax.axis_index("row") % 2 == 0
    both = jnp.stack([jnp.where(first, mine, other), jnp.where(first, other, mine)], axis=1)
    fac = both[:, :, :, :PIECE].transpose(0, 1, 3, 2, 4).reshape(TILE, col_count * width)
    feat = both[:, :, :4, PIECE:].reshape(TILE, width)
    return fac, feat


def body(features, factor_prev, panel_index):
    row_count = lax.axis_size("row")
    col_count = lax.axis_size("col")
    my_rows = features.shape[0] // col_count
    width = factor_prev.shape[1]
    panel_tile = panel_index[0]
    owner_row = panel_tile % row_count
    local_tile = panel_tile // row_count
    my_col = lax.axis_index("col")
    my_row = lax.axis_index("row")
    my_fac = lax.all_to_all(factor_prev.reshape(col_count, my_rows, width), "col", 0, 0, tiled=True)
    own_feat = lax.dynamic_slice_in_dim(features, local_tile * TILE, TILE, 0)
    own_fac = lax.dynamic_slice_in_dim(factor_prev, local_tile * TILE, TILE, 0)
    panel_fac, panel_feat = gather_panel(own_fac, own_feat, owner_row)
    columns = jnp.arange(TILE, dtype=jnp.int32)
    identity_mask = columns[:, None] == columns[None, :]
    diagonal_update = jnp.dot(panel_fac, panel_fac.T, preferred_element_type=jnp.float32)
    diagonal = kernel_block(panel_feat, panel_feat, identity_mask) - diagonal_update
    diagonal_factor = jnp.linalg.cholesky(diagonal)
    identity = jnp.eye(TILE, dtype=jnp.float32)
    inverse = lax.linalg.triangular_solve(diagonal_factor, identity, left_side=True, lower=True)
    my_feat = lax.dynamic_slice_in_dim(features, my_col * my_rows, my_rows, 0)
    tile_of = my_col * row_count + my_row
    self_pair = (tile_of == panel_tile) & identity_mask
    my_fac = my_fac.transpose(1, 0, 2).reshape(my_rows, col_count * width)
    update = jnp.dot(my_fac, panel_fac.T, preferred_element_type=jnp.float32)
    column_block = kernel_block(my_feat, panel_feat, self_pair) - update
    panel = jnp.dot(column_block, inverse.T, precision=lax.Precision.HIGHEST)
    panel = jnp.where(tile_of >= panel_tile, panel, jnp.float32(0.0))
    log_det = 2.0 * jnp.sum(jnp.log(jnp.diagonal(diagonal_factor))) / TILE
    return (panel, jnp.reshape(log_det, (1,)))


def solution(mesh):
    in_specs = (P("row", None), P("row", "col"), P())
    out_specs = (P(("row", "col"), None), P())
    return jax.shard_map(body, mesh=mesh, in_specs=in_specs, out_specs=out_specs, check_vma=False)
```

time: 376 us -> 159 us (0.42)
  the two profiles are of different devices: /device:TPU:24 before, /device:TPU:1 now
where the time goes in v1:
time: 159 us; the launch traced here: 158 us
  other arithmetic  60.4 us (38%)
  blocking collectives  35.7 us (22%)
  starting transfers between devices  23.7 us (15%)
  local copies, waits for them, and re-layouts  17.6 us (11%)
  waiting for transfers between devices  9.64 us (6%)
  matrix products  6.18 us (4%)
  between operations  4.73 us (3%)
    another operation x6, other arithmetic, body(): diagonal_factor = jnp.linalg.cholesky(diagonal)  34.1 us
    all_to_all x1, blocking collectives, gather_panel(): lax.all_to_all(jnp.broadcast_to(slot, (col_count, SLOT, width)), 'col', 0...  25.1 us
    another operation x3, other arithmetic, body(): lax.linalg.triangular_solve(diagonal_factor, identity, left_side=True, lo...  20.5 us
    all_to_all x1, blocking collectives, gather_panel(): lax.all_to_all(copies, 'row', 0, 0, tiled=True, axis_index_groups=over_x)  10.6 us
    all_to_all x1, starting transfers between devices, gather_panel(): got = lax.all_to_all(send, 'row', 0, 0, tiled=True)  10.4 us
    all_to_all x1, waiting for transfers between devices, gather_panel(): got = lax.all_to_all(send, 'row', 0, 0, tiled=True)  9.63 us
    all_to_all x1, starting transfers between devices, body(): lax.all_to_all(factor_prev.reshape(col_count, my_rows, width), 'col', 0,...  6.96 us
    ppermute x1, starting transfers between devices, gather_panel(): other = lax.ppermute(mine, 'row', [(i, i ^ 1) for i in range(32)])  6.38 us
  transfers between devices with their start and end apart: 3, of which 1 were waited for; matrix products, arithmetic and copies ran while one was open for 48% of the time, Pallas kernels for 0%

profile of v1, /device:TPU:1, one launch (start us, length us, event | category | flops | bytes accessed | tf_op | source)
XLA Modules:
  0.0 157.9 jit_solution(203356452533762516)
XLA Ops:
  1.3 0.8 constant_dynamic-slice_fusion.1
  2.2 0.8 constant_dynamic-slice_fusion.2
  3.0 0.8 maximum_maximum_fusion
  3.8 10.4 %all-to-all-start = ((bf16[32,40,128]{2,1,0:T(8,128)(2,1)}), bf16[32,40,128]{2,1,0:T(8,128)(2,1)S(1)}, u32[]{:S(2)}, u32[]{:S(2)}) async-start(bf16[32,40,128]{2,1,0:T(8,128)(2,1)} %maximum_maximum_fusion), calls=%async_computation | async-start | bytes 655360 | tf_op jit(solution)/shard_map/all_to_all | solution.py:35
  14.2 9.6 %all-to-all-done = bf16[32,40,128]{2,1,0:T(8,128)(2,1)S(1)} async-done(((bf16[32,40,128]{2,1,0:T(8,128)(2,1)}), bf16[32,40,128]{2,1,0:T(8,128)(2,1)S(1)}, u32[]{:S(2)}, u32[]{:S(2)}) %all-to-all-start) | async-done | bytes 327712 | tf_op jit(solution)/shard_map/all_to_all | solution.py:35
  23.9 25.1 %all_to_all.20 = bf16[16,40,128]{2,1,0:T(8,128)(2,1)S(1)} all-to-all(bf16[16,40,128]{2,1,0:T(8,128)(2,1)S(1)} %broadcast_in_dim.42), channel_id=1, replica_groups=mesh['row'=32,'col'=16] {'col'}, dimensions={0} | all-to-all | bytes 327680 | tf_op jit(solution)/shard_map/all_to_all | solution.py:37
  49.1 10.6 %all_to_all.21 = bf16[4,16,40,128]{3,2,1,0:T(8,128)(2,1)S(1)} all-to-all(bf16[4,16,40,128]{3,2,1,0:T(8,128)(2,1)S(1)} %broadcast_in_dim.43), channel_id=1, replica_groups={{0,32,64,96},{16,48,80,112},{128,160,192,224},{144,176,208,240},{256,28..., dimensions={0} | all-to-all | bytes 1310720 | tf_op jit(solution)/shard_map/all_to_all | solution.py:40
  59.6 6.4 %collective-permute-start = (bf16[4,16,40,128]{3,2,1,0:T(8,128)(2,1)S(1)}, bf16[4,16,40,128]{3,2,1,0:T(8,128)(2,1)}, u32[]{:S(2)}, u32[]{:S(2)}) collective-permute-start(bf16[4,16,40,128]{3,2,1,0:T(8,128)(2,1)S(1)} %all_to_all.21), channel_id=1, source_target_pairs={{0,16},{16,0},{32,48},{48,32},{64,80},{80,64},{96,112},{112,96},{1... | collective-permute-start | bytes 1966088 | tf_op jit(solution)/shard_map/ppermute | solution.py:41
  66.0 7.0 %all-to-all-start.3 = ((bf16[16,256,128]{2,1,0:T(8,128)(2,1)}), bf16[16,256,128]{2,1,0:T(8,128)(2,1)S(1)}, u32[]{:S(2)}, u32[]{:S(2)}) async-start(bf16[16,256,128]{2,1,0:T(8,128)(2,1)} %bitcast.10), calls=%async_computation.3 | async-start | bytes 2097152 | tf_op jit(solution)/shard_map/all_to_all | solution.py:59
  73.0 0.8 copy.40
  73.8 0.8 copy.31
  74.6 0.9 multiply_reduce_fusion.1
  75.6 1.2 select_bitcast_fusion.1
  76.8 0.1 multiply_reduce_fusion
  76.9 0.2 convolution_multiply_fusion
  77.1 0.1 copy.36
  77.2 0.1 add.100
  77.3 1.0 fusion.18
  78.4 1.8 %copy.39 = f32[256,256]{1,0:T(8,128)} copy(f32[256,256]{0,1:T(8,128)} %get-tuple-element.30) | data formatting | bytes 524288 | tf_op jit(solution)/shard_map/neg | solution.py:23
  80.2 1.8 %copy.42 = f32[256,256]{1,0:T(8,128)} copy(f32[256,256]{0,1:T(8,128)} %get-tuple-element.31) | data formatting | bytes 524288 | tf_op jit(solution)/shard_map/sqrt | solution.py:22
  82.0 0.4 copy.33
  82.5 0.5 fusion.9
  83.0 0.5 copy-done
  83.5 0.1 copy.43
  83.6 0.3 copy-done.3
  83.9 1.0 fusion.25
  84.9 11.7 %cholesky.49 = f32[128,128]{1,0:T(8,128)S(1)} custom-call(f32[128,128]{1,0:T(8,128)S(1)} %cholesky.115), custom_call_target="Cholesky" | custom-call | tf_op jit(solution)/shard_map/jit(cholesky)/cholesky | solution.py:67
  96.7 9.8 %custom-call.14 = f32[1,128,128]{1,2,0:T(8,128)S(1)} custom-call(f32[1,128,128]{2,1,0:T(8,128)S(1)} %get-tuple-element.29), custom_call_target="InvertDiagBlocksLowerTriangular" | custom-call | tf_op jit(solution)/shard_map/jit(cholesky)/cholesky | solution.py:67
  106.5 0.2 constant_dynamic-update-slice_fusion
  106.7 0.3 convolution_subtract_fusion.1
  107.0 11.9 %cholesky.103 = f32[128,128]{1,0:T(8,128)S(1)} custom-call(f32[128,128]{1,0:T(8,128)S(1)} %convolution_subtract_fusion.1), custom_call_target="Cholesky" | custom-call | tf_op jit(solution)/shard_map/jit(cholesky)/cholesky | solution.py:67
  118.9 0.6 compare_reduce_fusion
  120.9 5.2 %while.1 = (s32[]{:T(128)}, f32[256,256]{1,0:T(8,128)S(1)}, s32[2,2]{1,0:T(2,128)S(1)}, f32[2,128,128]{2,1,0:T(8,128)}, s32[]{:T(128)}) while((s32[]{:T(128)}, f32[256,256]{1,0:T(8,128)S(1)}, s32[2,2]{1,0:T(2,128)S(1)}, f32[2,128,128]{2,1,0:T(8,128)}, s32[]{:T(128)}) %tuple.32), condition=%wide.while_cond, body=%wide.while_body.sunk | while | flops 2 | bytes 132705 | solution.py:69
  120.9 0.6 fusion.49
  121.5 2.0 %bitcast_dynamic-update-slice_fusion.2 = f32[2,128,128]{2,1,0:T(8,128)} fusion(f32[2,128,128]{2,1,0:T(8,128)} %get-tuple-element.74, s32[]{:T(128)} %get-tuple-element.71, f32[256,256]{1,0:T(8,128)S(1)} %get-tuple-element.77, s32[]{:T(128)} %bitcast.68, s32[]{:T(128)} %bitcast.69), kind=kLoop, calls=%fused_computation.1.clone.1 | loop fusion | bytes 132608 | tf_op jit(solution)/shard_map/triangular_solve
  123.5 0.6 fusion.49
  124.1 2.0 %bitcast_dynamic-update-slice_fusion.2 = f32[2,128,128]{2,1,0:T(8,128)} fusion(f32[2,128,128]{2,1,0:T(8,128)} %get-tuple-element.74, s32[]{:T(128)} %get-tuple-element.71, f32[256,256]{1,0:T(8,128)S(1)} %get-tuple-element.77, s32[]{:T(128)} %bitcast.68, s32[]{:T(128)} %bitcast.69), kind=kLoop, calls=%fused_computation.1.clone.1 | loop fusion | bytes 132608 | tf_op jit(solution)/shard_map/triangular_solve
  126.1 20.5 %custom-call.15 = f32[2,128,128]{1,2,0:T(8,128)S(1)} custom-call(f32[2,128,128]{2,1,0:T(8,128)} %get-tuple-element.9), custom_call_target="InvertDiagBlocksLowerTriangular" | custom-call | tf_op jit(solution)/shard_map/triangular_solve | solution.py:69
  146.6 0.1 copy.30
  146.8 2.3 %gather_fusion = f32[256]{0:T(256)S(1)} fusion(f32[256,256]{1,0:T(8,128)S(1)} %get-tuple-element.19, s32[256]{0:T(256)S(1)} %bitcast.76), kind=kCustom, calls=%fused_computation | custom fusion | bytes 4096 | tf_op jit(solution)/shard_map/jit(diagonal)/cond/branch_0_fun/gather | solution.py:78
  149.1 0.6 log_reduce_fusion
  150.4 0.3 fusion.28
  150.6 0.4 convolution_subtract_fusion
  151.0 0.3 fusion.31
  151.4 1.3 copy.34
  152.7 1.8 %convolution_bitcast_fusion = f32[256,256]{1,0:T(8,128)S(1)} fusion(bf16[256,2048]{0,1:T(8,128)(2,1)} %bitcast.82, bf16[32,8,16,128]{3,2,1,0:T(8,128)(2,1)S(1)} %bitcast.81), kind=kOutput, calls=%fused_computation.15 | convolution fusion | flops 268435456 | bytes 2359296 | tf_op jit(solution)/shard_map/dot_general | solution.py:74
  154.5 1.2 fusion.8
  155.7 1.1 convolution_select_fusion
  (28 shorter events, 0.5 us)
Async XLA Ops:
  3.8 20.1 %all-to-all-start = ((bf16[32,40,128]{2,1,0:T(8,128)(2,1)}), bf16[32,40,128]{2,1,0:T(8,128)(2,1)S(1)}, u32[]{:S(2)}, u32[]{:S(2)}) async-start(bf16[32,40,128]{2,1,0:T(8,128)(2,1)} %maximum_maximum_fusion), calls=%async_computation | async-start | bytes 655360 | tf_op jit(solution)/shard_map/all_to_all | solution.py:35
  59.6 16.0 %collective-permute-start = (bf16[4,16,40,128]{3,2,1,0:T(8,128)(2,1)S(1)}, bf16[4,16,40,128]{3,2,1,0:T(8,128)(2,1)}, u32[]{:S(2)}, u32[]{:S(2)}) collective-permute-start(bf16[4,16,40,128]{3,2,1,0:T(8,128)(2,1)S(1)} %all_to_all.21), channel_id=1, source_target_pairs={{0,16},{16,0},{32,48},{48,32},{64,80},{80,64},{96,112},{112,96},{1... | collective-permute-start | bytes 1966088 | tf_op jit(solution)/shard_map/ppermute | solution.py:41
  66.0 85.4 %all-to-all-start.3 = ((bf16[16,256,128]{2,1,0:T(8,128)(2,1)}), bf16[16,256,128]{2,1,0:T(8,128)(2,1)S(1)}, u32[]{:S(2)}, u32[]{:S(2)}) async-start(bf16[16,256,128]{2,1,0:T(8,128)(2,1)} %bitcast.10), calls=%async_computation.3 | async-start | bytes 2097152 | tf_op jit(solution)/shard_map/all_to_all | solution.py:59
  82.5 1.0 copy-start
  82.5 1.1 copy-start.2
  82.5 1.4 copy-start.3
  151.4 1.3 copy-start.1
  152.7 1.8 %copy-start.4 = (pred[256,256]{1,0:T(32,128)(4,1)S(1)}, pred[256,256]{1,0:T(32,128)(4,1)}, u32[]{:S(2)}) copy-start(pred[256,256]{1,0:T(32,128)(4,1)} %copy.31) | copy-start | bytes 196612

commit v2 on v1

v2 whole, which is shorter than its diff:
```python
import jax
import jax.numpy as jnp
from jax import lax
from jax.experimental import pallas as pl
from jax.experimental.pallas import tpu as pltpu
from jax.sharding import PartitionSpec as P

TILE = 256
FEAT = 128
NUGGET = 4.0
RANGE = 8.0
CHUNKS = 8
PIECE = TILE // CHUNKS
FEAT_PIECE = 8
BLOCK = 32
SUB = 8
LANES = 128
VMEM_LIMIT = 40 * 2**20


def tile_kernel(row_feat, panel_feat, self_pair):
    row_wide = row_feat.astype(jnp.float32)
    panel_wide = panel_feat.astype(jnp.float32)
    row_square = jnp.sum(row_wide * row_wide, axis=1, keepdims=True)
    square = panel_wide * panel_wide
    high = square.astype(jnp.bfloat16)
    low = (square - high.astype(jnp.float32)).astype(jnp.bfloat16)
    ones = jnp.ones((SUB, panel_feat.shape[1]), jnp.bfloat16)
    panel_square = (dot_last(ones, high) + dot_last(ones, low))[:1, :]
    cross_term = dot_last(row_feat, panel_feat)
    squared = jnp.maximum(row_square + panel_square - 2.0 * cross_term, 0.0)
    distance = jnp.where(self_pair, 0.0, jnp.sqrt(squared))
    return jnp.exp(-distance / RANGE) + jnp.where(self_pair, NUGGET, 0.0)


def dot_last(a, b):
    return lax.dot_general(a, b, (((1,), (1,)), ((), ())), preferred_element_type=jnp.float32)


def split3(a):
    high = a.astype(jnp.bfloat16)
    rest = a - high.astype(jnp.float32)
    mid = rest.astype(jnp.bfloat16)
    low = (rest - mid.astype(jnp.float32)).astype(jnp.bfloat16)
    return high, mid, low


def factor_rows(work, inverse, block, pivots, sub, lane, lane_wide):
    count = BLOCK // SUB
    begin = block * BLOCK
    base = begin // LANES * LANES
    diag, rows = [], []
    for i in range(count):
        row = work[begin + i * SUB : begin + (i + 1) * SUB, :]
        diag.append(row[:, base : base + LANES])
        inside = (lane_wide >= begin) & (lane_wide < begin + BLOCK)
        eye = lane_wide == begin + i * SUB + lax.broadcasted_iota(jnp.int32, (SUB, TILE), 0)
        rows.append(jnp.where(inside, eye.astype(jnp.float32), row))
    for j in range(count):
        first = begin - base + j * SUB
        column = [
            [jnp.broadcast_to(diag[i][:, first + k : first + k + 1], (SUB, LANES)) for k in range(SUB)]
            for i in range(j, count)
        ]
        pivot = jnp.ones((SUB, LANES), jnp.float32)
        for k in range(SUB):
            value = jnp.broadcast_to(column[0][k][k : k + 1, :], (SUB, LANES))
            recip = 1.0 / value
            pivot = jnp.where(sub == k, value, pivot)
            factor = [c[k] * recip for c in column]
            factor[0] = jnp.where(sub > k, factor[0], 0.0)
            for m in range(k + 1, SUB):
                other = jnp.broadcast_to(column[0][k][m : m + 1, :], (SUB, LANES))
                for i in range(len(column)):
                    column[i][m] = column[i][m] - factor[i] * other
            row_k = jnp.broadcast_to(rows[j][k : k + 1, :], (SUB, TILE))
            diag_k = jnp.broadcast_to(diag[j][k : k + 1, :], (SUB, LANES))
            for i in range(len(column)):
                rows[j + i] = rows[j + i] - jnp.concatenate([factor[i], factor[i]], axis=1) * row_k
                diag[j + i] = diag[j + i] - factor[i] * diag_k
        scale = 1.0 / jnp.sqrt(pivot)
        pivots = jnp.where(lane == block * count + j, pivot, pivots)
        rows[j] = rows[j] * jnp.concatenate([scale, scale], axis=1)
    whole = jnp.concatenate(rows, axis=0)
    inverse[begin : begin + BLOCK, :] = jnp.where(lane_wide < begin + BLOCK, whole, 0.0)
    return whole, pivots


def factor_tile(work, inverse):
    sub = lax.broadcasted_iota(jnp.int32, (SUB, LANES), 0)
    lane = lax.broadcasted_iota(jnp.int32, (SUB, LANES), 1)
    lane_wide = lax.broadcasted_iota(jnp.int32, (1, TILE), 1)
    pivots = jnp.ones((SUB, LANES), jnp.float32)
    for block in range(TILE // BLOCK):
        whole, pivots = factor_rows(work, inverse, block, pivots, sub, lane, lane_wide)
        end = (block + 1) * BLOCK
        if end == TILE:
            break
        base = end // LANES * LANES
        high, mid, low = split3(whole)
        left = jnp.concatenate([p[:, base:] for p in (high, high, mid, high, low, mid)], axis=0)
        right = jnp.concatenate([high, mid, high, low, high, mid], axis=0)
        update = lax.dot_general(left, right, (((0,), (0,)), ((), ())), preferred_element_type=jnp.float32)
        old = jnp.where((lane_wide >= end - BLOCK) & (lane_wide < end), 0.0, work[end:, :])
        work[end:, :] = old - update[end - base :, :]
    return jnp.sum(jnp.log(pivots)) / TILE


def diagonal_kernel(core, mine, other, inverse, log_det, panel_fac, panel_feat, work):
    layers = panel_fac.shape[1] // LANES
    for c in range(2):

        def place(source, c=c):
            for x in range(CHUNKS // 2):
                begin = (x * 2 + c) * PIECE
                for z in range(layers):
                    panel_fac[begin : begin + PIECE, z * LANES : (z + 1) * LANES] = source[
                        x, z * PIECE : (z + 1) * PIECE, :
                    ]
                panel_feat[begin : begin + PIECE, :] = source[x, layers * PIECE :, :]

        pl.when(core[0] == c)(lambda: place(mine))
        pl.when(core[0] != c)(lambda: place(other))
    row = lax.broadcasted_iota(jnp.int32, (TILE, TILE), 0)
    col = lax.broadcasted_iota(jnp.int32, (TILE, TILE), 1)
    feat = panel_feat[...]
    fac = panel_fac[...]
    work[...] = tile_kernel(feat, feat, row == col) - dot_last(fac, fac)
    log_det[...] = jnp.full((1, LANES), factor_tile(work, inverse), jnp.float32)


def panel_kernel(where, feat, fac, panel_feat, panel_fac, inverse, panel):
    tile_of = where[1]
    panel_tile = where[2]
    row = lax.broadcasted_iota(jnp.int32, (TILE, TILE), 0)
    col = lax.broadcasted_iota(jnp.int32, (TILE, TILE), 1)
    self_pair = (row == col) & (tile_of == panel_tile)
    rows = jnp.concatenate([fac[z] for z in range(fac.shape[0])], axis=1)
    update = dot_last(rows, panel_fac[...])
    block = tile_kernel(feat[...], panel_feat[...], self_pair) - update
    result = lax.dot_general(
        block,
        inverse[...],
        (((1,), (1,)), ((), ())),
        precision=lax.Precision.HIGHEST,
        preferred_element_type=jnp.float32,
    )
    panel[...] = jnp.where(tile_of >= panel_tile, result, 0.0)


def gather_panel(own_fac, own_feat, owner_row):
    width = own_fac.shape[1]
    col_count = lax.axis_size("col")
    my_col = lax.axis_index("col")
    fac_chunks = own_fac.reshape(CHUNKS, PIECE, width)
    feat_chunks = own_feat.reshape(CHUNKS, 4, FEAT_PIECE, width)
    feat_chunks = lax.dynamic_index_in_dim(feat_chunks, my_col % 4, 1, keepdims=False)
    slots = jnp.concatenate([fac_chunks, feat_chunks], axis=1)
    send = jnp.concatenate([slots] * 4, axis=0)
    got = lax.all_to_all(send, "row", 0, 0, tiled=True)
    slot = lax.dynamic_index_in_dim(got, owner_row, 0, keepdims=True)
    layers = lax.all_to_all(jnp.broadcast_to(slot, (col_count,) + slot.shape[1:]), "col", 0, 0, tiled=True)
    over_x = [[(y * 4 + x) * 2 + c for x in range(4)] for y in range(4) for c in range(2)]
    chunk = jnp.concatenate(
        [layers[:, :PIECE].reshape(col_count * PIECE, width), layers[:4, PIECE:].reshape(PIECE, width)], axis=0
    )
    copies = jnp.broadcast_to(chunk[None], (4,) + chunk.shape)
    mine = lax.all_to_all(copies, "row", 0, 0, tiled=True, axis_index_groups=over_x)
    other = lax.ppermute(mine, "row", [(i, i ^ 1) for i in range(32)])
    return mine, other


def body(features, factor_prev, panel_index):
    row_count = lax.axis_size("row")
    col_count = lax.axis_size("col")
    my_rows = features.shape[0] // col_count
    width = factor_prev.shape[1]
    panel_tile = panel_index[0]
    owner_row = panel_tile % row_count
    local_tile = panel_tile // row_count
    my_col = lax.axis_index("col")
    my_row = lax.axis_index("row")
    my_fac = lax.all_to_all(factor_prev.reshape(col_count, my_rows, width), "col", 0, 0, tiled=True)
    own_feat = lax.dynamic_slice_in_dim(features, local_tile * TILE, TILE, 0)
    own_fac = lax.dynamic_slice_in_dim(factor_prev, local_tile * TILE, TILE, 0)
    mine, other = gather_panel(own_fac, own_feat, owner_row)
    vmem = pl.BlockSpec(memory_space=pltpu.VMEM)
    smem = pl.BlockSpec(memory_space=pltpu.SMEM)
    inverse, log_det, panel_fac, panel_feat = pl.pallas_call(
        diagonal_kernel,
        out_shape=(
            jax.ShapeDtypeStruct((TILE, TILE), jnp.float32),
            jax.ShapeDtypeStruct((1, LANES), jnp.float32),
            jax.ShapeDtypeStruct((TILE, col_count * width), jnp.bfloat16),
            jax.ShapeDtypeStruct((TILE, FEAT), jnp.bfloat16),
        ),
        in_specs=[smem, vmem, vmem],
        out_specs=(vmem, vmem, vmem, vmem),
        scratch_shapes=[pltpu.VMEM((TILE, TILE), jnp.float32)],
        compiler_params=pltpu.CompilerParams(vmem_limit_bytes=VMEM_LIMIT),
        cost_estimate=pl.CostEstimate(flops=10**10, bytes_accessed=4 * 10**6, transcendentals=10**5),
    )((my_row % 2).reshape(1), mine, other)
    tile_of = my_col * row_count + my_row
    where = jnp.stack([my_col, tile_of, panel_tile]).astype(jnp.int32)
    whole = lambda *shape: pl.BlockSpec(shape, lambda i, where: (0,) * len(shape))
    panel = pl.pallas_call(
        panel_kernel,
        out_shape=jax.ShapeDtypeStruct((TILE, TILE), jnp.float32),
        grid_spec=pltpu.PrefetchScalarGridSpec(
            num_scalar_prefetch=1,
            grid=(1,),
            in_specs=[
                pl.BlockSpec((TILE, FEAT), lambda i, where: (where[0], 0)),
                whole(col_count, my_rows, width),
                whole(TILE, FEAT),
                whole(TILE, col_count * width),
                whole(TILE, TILE),
            ],
            out_specs=whole(TILE, TILE),
        ),
        compiler_params=pltpu.CompilerParams(vmem_limit_bytes=VMEM_LIMIT),
        cost_estimate=pl.CostEstimate(flops=10**9, bytes_accessed=4 * 10**6, transcendentals=10**5),
    )(where, features, my_fac, panel_feat, panel_fac, inverse)
    return (panel, log_det[0, :1])


def solution(mesh):
    in_specs = (P("row", None), P("row", "col"), P())
    out_specs = (P(("row", "col"), None), P())
    return jax.shard_map(body, mesh=mesh, in_specs=in_specs, out_specs=out_specs, check_vma=False)
```

time: 159 us -> 120 us (0.75)
  the two profiles are of different devices: /device:TPU:1 before, /device:TPU:24 now
where the time goes in v2:
time: 120 us; the launch traced here: 119 us
  waiting for transfers between devices  42 us (35%)
  blocking collectives  39 us (32%)
  starting transfers between devices  18.5 us (15%)
  Pallas kernels  12 us (10%)
  local copies, waits for them, and re-layouts  4.74 us (4%)
  between operations  1.42 us (1%)
    all_to_all x1, waiting for transfers between devices, body(): lax.all_to_all(factor_prev.reshape(col_count, my_rows, width), 'col', 0,...  32.8 us
    all_to_all x1, blocking collectives, gather_panel(): lax.all_to_all(jnp.broadcast_to(slot, (col_count,) + slot.shape[1:]), 'co...  27.9 us
    all_to_all x1, blocking collectives, gather_panel(): lax.all_to_all(copies, 'row', 0, 0, tiled=True, axis_index_groups=over_x)  11.2 us
    pallas_call x1, Pallas kernels, body(): pl.pallas_call(diagonal_kernel, out_shape=(jax.ShapeDtypeStruct((TILE, TI...  9.52 us
    all_to_all x1, starting transfers between devices, gather_panel(): got = lax.all_to_all(send, 'row', 0, 0, tiled=True)  9.28 us
    all_to_all x1, waiting for transfers between devices, gather_panel(): got = lax.all_to_all(send, 'row', 0, 0, tiled=True)  7.34 us
    all_to_all x1, starting transfers between devices, body(): lax.all_to_all(factor_prev.reshape(col_count, my_rows, width), 'col', 0,...  7.34 us
    unnamed x10, local copies, waits for them, and re-layouts  2.93 us
  transfers between devices with their start and end apart: 3, of which 3 were waited for; matrix products, arithmetic and copies ran while one was open for 0% of the time, Pallas kernels for 8%

profile of v2, /device:TPU:24, one launch (start us, length us, event | category | flops | bytes accessed | tf_op | source)
XLA Modules:
  0.0 118.5 jit_solution(17988537268350033840)
XLA Ops:
  1.3 0.8 constant_dynamic-slice_fusion
  2.2 0.8 constant_dynamic-slice_fusion.1
  3.0 0.8 maximum_maximum_fusion
  3.8 9.3 %all-to-all-start.1 = ((bf16[32,40,128]{2,1,0:T(8,128)(2,1)}), bf16[32,40,128]{2,1,0:T(8,128)(2,1)S(1)}, u32[]{:S(2)}, u32[]{:S(2)}) async-start(bf16[32,40,128]{2,1,0:T(8,128)(2,1)} %maximum_maximum_fusion), calls=%async_computation.1 | async-start | bytes 655360 | tf_op jit(solution)/shard_map/all_to_all | solution.py:160
  13.1 7.3 %all-to-all-done.1 = bf16[32,40,128]{2,1,0:T(8,128)(2,1)S(1)} async-done(((bf16[32,40,128]{2,1,0:T(8,128)(2,1)}), bf16[32,40,128]{2,1,0:T(8,128)(2,1)S(1)}, u32[]{:S(2)}, u32[]{:S(2)}) %all-to-all-start.1) | async-done | bytes 327712 | tf_op jit(solution)/shard_map/all_to_all | solution.py:160
  20.5 27.9 %all_to_all.20 = bf16[16,40,128]{2,1,0:T(8,128)(2,1)S(1)} all-to-all(bf16[16,40,128]{2,1,0:T(8,128)(2,1)S(1)} %broadcast_in_dim.14), channel_id=1, replica_groups=mesh['row'=32,'col'=16] {'col'}, dimensions={0} | all-to-all | bytes 327680 | tf_op jit(solution)/shard_map/all_to_all | solution.py:162
  48.4 0.1 broadcast_in_dim.15
  48.5 11.2 %all_to_all.21.mine = bf16[4,544,128]{2,1,0:T(8,128)(2,1)S(1)} all-to-all(bf16[4,544,128]{2,1,0:T(8,128)(2,1)S(1)} %broadcast_in_dim.15), channel_id=1, replica_groups={{0,32,64,96},{16,48,80,112},{128,160,192,224},{144,176,208,240},{256,28..., dimensions={0} | all-to-all | bytes 1114112 | tf_op jit(solution)/shard_map/all_to_all | solution.py:168
  59.6 0.0 copy-start.1
  59.6 7.3 %all-to-all-start = ((bf16[16,256,128]{2,1,0:T(8,128)(2,1)}), bf16[16,256,128]{2,1,0:T(8,128)(2,1)S(1)}, u32[]{:S(2)}, u32[]{:S(2)}) async-start(bf16[16,256,128]{2,1,0:T(8,128)(2,1)} %bitcast.2), calls=%async_computation | async-start | bytes 2097152 | tf_op jit(solution)/shard_map/all_to_all | solution.py:183
  67.0 0.0 copy-done.1
  67.0 1.9 %collective-permute-start = (bf16[4,544,128]{2,1,0:T(8,128)(2,1)S(1)}, bf16[4,544,128]{2,1,0:T(8,128)(2,1)S(1)}, u32[]{:S(2)}, u32[]{:S(2)}) collective-permute-start(bf16[4,544,128]{2,1,0:T(8,128)(2,1)S(1)} %all_to_all.21.mine), channel_id=1, source_target_pairs={{0,16},{16,0},{32,48},{48,32},{64,80},{80,64},{96,112},{112,96},{1... | collective-permute-start | bytes 1671176 | tf_op jit(solution)/shard_map/ppermute | solution.py:169
  68.9 0.1 pad_add_fusion.where
  69.0 1.8 %collective-permute-done.other = bf16[4,544,128]{2,1,0:T(8,128)(2,1)S(1)} collective-permute-done((bf16[4,544,128]{2,1,0:T(8,128)(2,1)S(1)}, bf16[4,544,128]{2,1,0:T(8,128)(2,1)S(1)}, u32[]{:S(2)}, u32[]{:S(2)}) %collective-permute-start) | collective-permute-done | bytes 557088 | tf_op jit(solution)/shard_map/ppermute | solution.py:169
  70.8 0.0 copy-start.3
  70.8 0.8 copy-done.3
  71.7 0.0 copy-start.2
  71.7 1.1 copy-done.2
  72.7 0.0 copy-start.4
  72.7 1.1 copy-done.4
  73.8 0.0 copy-start
  73.8 9.5 %shard_map.50 = (f32[256,256]{1,0:T(8,128)S(1)}, f32[1,128]{1,0:T(1,128)}, bf16[256,2048]{1,0:T(8,128)(2,1)S(1)}, bf16[256,128]{1,0:T(8,128)(2,1)S(1)}) custom-call(s32[1]{0:T(128)} %bitcast.3.core, bf16[4,544,128]{2,1,0:T(8,128)(2,1)S(1)} %copy-done.2, bf16[4,544,128]{2,1,0:T(8,128)(2,1)S(1)} %copy-done.4), custom_call_target="tpu_custom_call" | custom-call | flops 10000000000 | bytes 4000000 | tf_op jit(solution)/shard_map/pallas_call | solution.py:189
  83.3 32.8 %all-to-all-done.fac = bf16[16,256,128]{2,1,0:T(8,128)(2,1)S(1)} async-done(((bf16[16,256,128]{2,1,0:T(8,128)(2,1)}), bf16[16,256,128]{2,1,0:T(8,128)(2,1)S(1)}, u32[]{:S(2)}, u32[]{:S(2)}) %all-to-all-start) | async-done | bytes 1048608 | tf_op jit(solution)/shard_map/all_to_all | solution.py:183
  116.1 0.0 copy-done
  116.1 2.4 %shard_map.51 = f32[256,256]{1,0:T(8,128)} custom-call(s32[3]{0:T(128)S(1)} %pad_add_fusion.where, bf16[4096,128]{1,0:T(8,128)(2,1)S(1)} %copy-done, bf16[16,256,128]{2,1,0:T(8,128)(2,1)S(1)} %all-to-all-done.fac, bf16[256,128]{1,0:T(8,128)(2,1)S(1)} %get-tuple-element.6.panel_feat, bf16[256,2048]{1,0:T(8,128)(2,1)S(1)} %get-tuple-element.7.panel_fac, ...), custom_call_target="tpu_custom_call" | custom-call | flops 1000000000 | bytes 4000000 | tf_op jit(solution)/shard_map/pallas_call | solution.py:206
  (6 shorter events, 0.1 us)
Async XLA Ops:
  3.8 16.6 %all-to-all-start.1 = ((bf16[32,40,128]{2,1,0:T(8,128)(2,1)}), bf16[32,40,128]{2,1,0:T(8,128)(2,1)S(1)}, u32[]{:S(2)}, u32[]{:S(2)}) async-start(bf16[32,40,128]{2,1,0:T(8,128)(2,1)} %maximum_maximum_fusion), calls=%async_computation.1 | async-start | bytes 655360 | tf_op jit(solution)/shard_map/all_to_all | solution.py:160
  59.6 7.4 %copy-start.1 = (bf16[4,544,128]{2,1,0:T(8,128)(2,1)}, bf16[4,544,128]{2,1,0:T(8,128)(2,1)S(1)}, u32[]{:S(2)}) copy-start(bf16[4,544,128]{2,1,0:T(8,128)(2,1)S(1)} %all_to_all.21.mine) | copy-start | bytes 1671172
  59.6 56.5 %all-to-all-start = ((bf16[16,256,128]{2,1,0:T(8,128)(2,1)}), bf16[16,256,128]{2,1,0:T(8,128)(2,1)S(1)}, u32[]{:S(2)}, u32[]{:S(2)}) async-start(bf16[16,256,128]{2,1,0:T(8,128)(2,1)} %bitcast.2), calls=%async_computation | async-start | bytes 2097152 | tf_op jit(solution)/shard_map/all_to_all | solution.py:183
  67.0 3.9 %collective-permute-start = (bf16[4,544,128]{2,1,0:T(8,128)(2,1)S(1)}, bf16[4,544,128]{2,1,0:T(8,128)(2,1)S(1)}, u32[]{:S(2)}, u32[]{:S(2)}) collective-permute-start(bf16[4,544,128]{2,1,0:T(8,128)(2,1)S(1)} %all_to_all.21.mine), channel_id=1, source_target_pairs={{0,16},{16,0},{32,48},{48,32},{64,80},{80,64},{96,112},{112,96},{1... | collective-permute-start | bytes 1671176 | tf_op jit(solution)/shard_map/ppermute | solution.py:169
  70.8 0.8 copy-start.3
  71.7 1.1 copy-start.2
  72.7 1.1 copy-start.4
  73.8 42.3 %copy-start = (bf16[4096,128]{1,0:T(8,128)(2,1)S(1)}, bf16[4096,128]{1,0:T(8,128)(2,1)}, u32[]{:S(2)}) copy-start(bf16[4096,128]{1,0:T(8,128)(2,1)} %feat.1) | copy-start | bytes 3145732

commit v3 on v2

--- a/solution.py
+++ b/solution.py
@@ -1,5 +1,6 @@
 import jax
 import jax.numpy as jnp
+import numpy as np
 from jax import lax
 from jax.experimental import pallas as pl
 from jax.experimental.pallas import tpu as pltpu
@@ -9,9 +10,8 @@
 FEAT = 128
 NUGGET = 4.0
 RANGE = 8.0
-CHUNKS = 8
+CHUNKS = 32
 PIECE = TILE // CHUNKS
-FEAT_PIECE = 8
 BLOCK = 32
 SUB = 8
 LANES = 128
@@ -106,21 +106,13 @@
     return jnp.sum(jnp.log(pivots)) / TILE
 
 
-def diagonal_kernel(core, mine, other, inverse, log_det, panel_fac, panel_feat, work):
-    layers = panel_fac.shape[1] // LANES
-    for c in range(2):
-
-        def place(source, c=c):
-            for x in range(CHUNKS // 2):
-                begin = (x * 2 + c) * PIECE
-                for z in range(layers):
-                    panel_fac[begin : begin + PIECE, z * LANES : (z + 1) * LANES] = source[
-                        x, z * PIECE : (z + 1) * PIECE, :
-                    ]
-                panel_feat[begin : begin + PIECE, :] = source[x, layers * PIECE :, :]
-
-        pl.when(core[0] == c)(lambda: place(mine))
-        pl.when(core[0] != c)(lambda: place(other))
+def send_kernel(panel_index, features, factor_prev, send):
+    fac = factor_prev[...].astype(jnp.float32).reshape(CHUNKS, PIECE, LANES)
+    feat = features[...].astype(jnp.float32).reshape(CHUNKS, PIECE, LANES)
+    send[...] = jnp.concatenate([fac, feat], axis=1).astype(jnp.bfloat16)
+
+
+def diagonal_kernel(panel_fac, panel_feat, inverse, log_det, work):
     row = lax.broadcasted_iota(jnp.int32, (TILE, TILE), 0)
     col = lax.broadcasted_iota(jnp.int32, (TILE, TILE), 1)
     feat = panel_feat[...]
@@ -148,26 +140,32 @@
     panel[...] = jnp.where(tile_of >= panel_tile, result, 0.0)
 
 
-def gather_panel(own_fac, own_feat, owner_row):
-    width = own_fac.shape[1]
+def groups_of(axis):
+    index = np.arange(32).reshape(4, 4, 2)
+    return np.moveaxis(index, {"y": 0, "x": 1}[axis], 2).reshape(-1, 4).tolist()
+
+
+def gather_panel(send, owner_row):
+    width = send.shape[2]
     col_count = lax.axis_size("col")
-    my_col = lax.axis_index("col")
-    fac_chunks = own_fac.reshape(CHUNKS, PIECE, width)
-    feat_chunks = own_feat.reshape(CHUNKS, 4, FEAT_PIECE, width)
-    feat_chunks = lax.dynamic_index_in_dim(feat_chunks, my_col % 4, 1, keepdims=False)
-    slots = jnp.concatenate([fac_chunks, feat_chunks], axis=1)
-    send = jnp.concatenate([slots] * 4, axis=0)
     got = lax.all_to_all(send, "row", 0, 0, tiled=True)
-    slot = lax.dynamic_index_in_dim(got, owner_row, 0, keepdims=True)
-    layers = lax.all_to_all(jnp.broadcast_to(slot, (col_count,) + slot.shape[1:]), "col", 0, 0, tiled=True)
-    over_x = [[(y * 4 + x) * 2 + c for x in range(4)] for y in range(4) for c in range(2)]
-    chunk = jnp.concatenate(
-        [layers[:, :PIECE].reshape(col_count * PIECE, width), layers[:4, PIECE:].reshape(PIECE, width)], axis=0
-    )
-    copies = jnp.broadcast_to(chunk[None], (4,) + chunk.shape)
-    mine = lax.all_to_all(copies, "row", 0, 0, tiled=True, axis_index_groups=over_x)
+    slot = lax.dynamic_index_in_dim(got, owner_row, 0, keepdims=False)
+    copies = jnp.broadcast_to(slot[None, :PIECE], (col_count, PIECE, width))
+    layers = lax.all_to_all(copies, "col", 0, 0, tiled=True)
+    return layers, slot[PIECE:]
+
+
+def gather_chunks(layers, feat):
+    col_count, _, width = layers.shape
+    chunk = jnp.concatenate([layers.reshape(col_count * PIECE, width), feat], axis=0)
+    over_x = lax.all_gather(chunk, "row", axis=0, axis_index_groups=groups_of("x"))
+    mine = lax.all_gather(over_x, "row", axis=0, axis_index_groups=groups_of("y"))
     other = lax.ppermute(mine, "row", [(i, i ^ 1) for i in range(32)])
-    return mine, other
+    first = lax.axis_index("row") % 2 == 0
+    both = jnp.stack([jnp.where(first, mine, other), jnp.where(first, other, mine)], axis=2)
+    fac = both[:, :, :, : col_count * PIECE].reshape(CHUNKS, col_count, PIECE, width)
+    fac = fac.transpose(0, 2, 1, 3).reshape(TILE, col_count * width)
+    return fac, both[:, :, :, col_count * PIECE :].reshape(TILE, width)
 
 
 def body(features, factor_prev, panel_index):
@@ -177,29 +175,37 @@
     width = factor_prev.shape[1]
     panel_tile = panel_index[0]
     owner_row = panel_tile % row_count
-    local_tile = panel_tile // row_count
     my_col = lax.axis_index("col")
     my_row = lax.axis_index("row")
-    my_fac = lax.all_to_all(factor_prev.reshape(col_count, my_rows, width), "col", 0, 0, tiled=True)
-    own_feat = lax.dynamic_slice_in_dim(features, local_tile * TILE, TILE, 0)
-    own_fac = lax.dynamic_slice_in_dim(factor_prev, local_tile * TILE, TILE, 0)
-    mine, other = gather_panel(own_fac, own_feat, owner_row)
+    tiles = factor_prev.reshape(col_count, my_rows, width)
+    tile_rows = pl.BlockSpec((TILE, LANES), lambda i, index: (lax.div(index[0], row_count), 0))
+    send = pl.pallas_call(
+        send_kernel,
+        out_shape=jax.ShapeDtypeStruct((CHUNKS, 2 * PIECE, LANES), jnp.bfloat16),
+        grid_spec=pltpu.PrefetchScalarGridSpec(
+            num_scalar_prefetch=1,
+            grid=(1,),
+            in_specs=[tile_rows, tile_rows],
+            out_specs=pl.BlockSpec((CHUNKS, 2 * PIECE, LANES), lambda i, index: (0, 0, 0)),
+        ),
+    )(panel_index, features, factor_prev)
+    layers, feat_rows = gather_panel(send, owner_row)
+    tiles, layers = lax.optimization_barrier((tiles, layers))
+    my_fac = lax.all_to_all(tiles, "col", 0, 0, tiled=True)
+    panel_fac, panel_feat = gather_chunks(layers, feat_rows)
     vmem = pl.BlockSpec(memory_space=pltpu.VMEM)
-    smem = pl.BlockSpec(memory_space=pltpu.SMEM)
-    inverse, log_det, panel_fac, panel_feat = pl.pallas_call(
+    inverse, log_det = pl.pallas_call(
         diagonal_kernel,
         out_shape=(
             jax.ShapeDtypeStruct((TILE, TILE), jnp.float32),
             jax.ShapeDtypeStruct((1, LANES), jnp.float32),
-            jax.ShapeDtypeStruct((TILE, col_count * width), jnp.bfloat16),
-            jax.ShapeDtypeStruct((TILE, FEAT), jnp.bfloat16),
         ),
-        in_specs=[smem, vmem, vmem],
-        out_specs=(vmem, vmem, vmem, vmem),
+        in_specs=[vmem, vmem],
+        out_specs=(vmem, vmem),
         scratch_shapes=[pltpu.VMEM((TILE, TILE), jnp.float32)],
         compiler_params=pltpu.CompilerParams(vmem_limit_bytes=VMEM_LIMIT),
         cost_estimate=pl.CostEstimate(flops=10**10, bytes_accessed=4 * 10**6, transcendentals=10**5),
-    )((my_row % 2).reshape(1), mine, other)
+    )(panel_fac, panel_feat)
     tile_of = my_col * row_count + my_row
     where = jnp.stack([my_col, tile_of, panel_tile]).astype(jnp.int32)
     whole = lambda *shape: pl.BlockSpec(shape, lambda i, where: (0,) * len(shape))

time: 120 us -> 100 us (0.83)
  waiting for transfers between devices: 42 us -> 17.9 us
  blocking collectives: 39 us -> 50.9 us
  local copies, waits for them, and re-layouts: 4.74 us -> 0.02 us
  starting transfers between devices: 18.5 us -> 14.8 us
  Pallas kernels: 12 us -> 13.3 us
    all_gather x0 -> x2, blocking collectives: none -> 25.2 us  [the longest x1 13.2 us: gather_chunks(): lax.all_gather(over_x, 'row', axis=0, axis_index_groups=groups_of('y'))]
    all_to_all x1, waiting for transfers between devices: 32.8 us -> 10.2 us  [body(): my_fac = lax.all_to_all(tiles, 'col', 0, 0, tiled=True)]
    all_to_all x2 -> x1, blocking collectives: 39 us -> 25.7 us  [gather_panel(): layers = lax.all_to_all(copies, 'col', 0, 0, tiled=True)]
    all_to_all x1, starting transfers between devices: 7.34 us -> 3.66 us  [body(): my_fac = lax.all_to_all(tiles, 'col', 0, 0, tiled=True)]
    unnamed x10 -> x2, local copies, waits for them, and re-layouts: 2.93 us -> 0.01 us
    dynamic_slice x2 -> x0, local copies, waits for them, and re-layouts: 1.69 us -> none  [the longest x1 0.85 us: body(): own_feat = lax.dynamic_slice_in_dim(features, local_tile * TILE, TILE, 0)]
    pallas_call x0 -> x1, Pallas kernels: none -> 1.55 us  [body(): pl.pallas_call(send_kernel, out_shape=jax.ShapeDtypeStruct((CHUNKS, 2 * P...]
    all_to_all x1, waiting for transfers between devices: 7.34 us -> 5.82 us  [gather_panel(): got = lax.all_to_all(send, 'row', 0, 0, tiled=True)]
  transfers between devices with their start and end apart: 3 -> 3, of which waited for: 3 -> 3; matrix products, arithmetic and copies ran while one was open for 0% -> 0% of each run, Pallas kernels for 8% -> 9%
where the time goes in v3:
time: 100 us; the launch traced here: 98.7 us
  blocking collectives  50.9 us (51%)
  waiting for transfers between devices  17.9 us (18%)
  starting transfers between devices  14.8 us (15%)
  Pallas kernels  13.3 us (13%)
  between operations  1.38 us (1%)
    all_to_all x1, blocking collectives, gather_panel(): layers = lax.all_to_all(copies, 'col', 0, 0, tiled=True)  25.7 us
    all_gather x1, blocking collectives, gather_chunks(): lax.all_gather(over_x, 'row', axis=0, axis_index_groups=groups_of('y'))  13.2 us
    all_gather x1, blocking collectives, gather_chunks(): lax.all_gather(chunk, 'row', axis=0, axis_index_groups=groups_of('x'))  12 us
    all_to_all x1, waiting for transfers between devices, body(): my_fac = lax.all_to_all(tiles, 'col', 0, 0, tiled=True)  10.2 us
    pallas_call x1, Pallas kernels, body(): pl.pallas_call(diagonal_kernel, out_shape=(jax.ShapeDtypeStruct((TILE, TI...  9.33 us
    all_to_all x1, starting transfers between devices, gather_panel(): got = lax.all_to_all(send, 'row', 0, 0, tiled=True)  9.27 us
    all_to_all x1, waiting for transfers between devices, gather_panel(): got = lax.all_to_all(send, 'row', 0, 0, tiled=True)  5.82 us
    all_to_all x1, starting transfers between devices, body(): my_fac = lax.all_to_all(tiles, 'col', 0, 0, tiled=True)  3.66 us
  transfers between devices with their start and end apart: 3, of which 3 were waited for; matrix products, arithmetic and copies ran while one was open for 0% of the time, Pallas kernels for 9%

profile of v3, /device:TPU:24, one launch (start us, length us, event | category | flops | bytes accessed | tf_op | source)
XLA Modules:
  0.0 98.7 jit_solution(14213623310217667858)
XLA Ops:
  1.3 1.6 %shard_map.50 = bf16[32,16,128]{2,1,0:T(8,128)(2,1)} custom-call(s32[1]{0:T(128)} %copy.7.panel_index, bf16[4096,128]{1,0:T(8,128)(2,1)} %feat.1, bf16[4096,128]{1,0:T(8,128)(2,1)} %factor_prev.1), custom_call_target="tpu_custom_call" | custom-call | tf_op jit(solution)/shard_map/pallas_call | solution.py:182
  2.8 9.3 %all-to-all-start = ((bf16[32,16,128]{2,1,0:T(8,128)(2,1)}), bf16[32,16,128]{2,1,0:T(8,128)(2,1)S(1)}, u32[]{:S(2)}, u32[]{:S(2)}) async-start(bf16[32,16,128]{2,1,0:T(8,128)(2,1)} %shard_map.50), calls=%async_computation | async-start | bytes 262144 | tf_op jit(solution)/shard_map/all_to_all | solution.py:151
  12.1 5.8 %all-to-all-done = bf16[32,16,128]{2,1,0:T(8,128)(2,1)S(1)} async-done(((bf16[32,16,128]{2,1,0:T(8,128)(2,1)}), bf16[32,16,128]{2,1,0:T(8,128)(2,1)S(1)}, u32[]{:S(2)}, u32[]{:S(2)}) %all-to-all-start) | async-done | bytes 131104 | tf_op jit(solution)/shard_map/all_to_all | solution.py:151
  18.0 25.7 %all_to_all.15 = bf16[16,8,128]{2,1,0:T(8,128)(2,1)S(1)} all-to-all(bf16[16,8,128]{2,1,0:T(8,128)(2,1)S(1)} %broadcast_in_dim.9), channel_id=1, replica_groups=mesh['row'=32,'col'=16] {'col'}, dimensions={0} | all-to-all | bytes 65536 | tf_op jit(solution)/shard_map/all_to_all | solution.py:154
  43.6 3.7 %all-to-all-start.2 = ((bf16[16,256,128]{2,1,0:T(8,128)(2,1)}), bf16[16,256,128]{2,1,0:T(8,128)(2,1)S(1)}, u32[]{:S(2)}, u32[]{:S(2)}) async-start(bf16[16,256,128]{2,1,0:T(8,128)(2,1)} %bitcast.2), calls=%async_computation.2 | async-start | bytes 2097152 | tf_op jit(solution)/shard_map/all_to_all | solution.py:194
  47.3 12.0 %all-gather = bf16[544,128]{1,0:T(8,128)(2,1)S(1)} all-gather(bf16[136,128]{1,0:T(8,128)(2,1)S(1)} %pad_maximum_fusion.2), channel_id=2, replica_groups={{0,32,64,96},{16,48,80,112},{128,160,192,224},{144,176,208,240},{256,28..., dimensions={0}, use_global_device_ids=true | all-gather | bytes 174080 | tf_op jit(solution)/shard_map/all_gather | solution.py:161
  59.3 13.2 %all-gather.1 = bf16[16,136,128]{2,1,0:T(8,128)(2,1)S(1)} all-gather(bf16[4,136,128]{2,1,0:T(8,128)(2,1)S(1)} %bitcast.34), channel_id=3, replica_groups={{0,128,256,384},{16,144,272,400},{32,160,288,416},{48,176,304,432},{64,..., dimensions={0}, use_global_device_ids=true | all-gather | bytes 696320 | tf_op jit(solution)/shard_map/all_gather | solution.py:162
  72.6 1.9 %collective-permute-start = (bf16[4,4,136,128]{3,2,1,0:T(8,128)(2,1)S(1)}, bf16[4,4,136,128]{3,2,1,0:T(8,128)(2,1)S(1)}, u32[]{:S(2)}, u32[]{:S(2)}) collective-permute-start(bf16[4,4,136,128]{3,2,1,0:T(8,128)(2,1)S(1)} %bitcast.32), channel_id=1, source_target_pairs={{0,16},{16,0},{32,48},{48,32},{64,80},{80,64},{96,112},{112,96},{1... | collective-permute-start | bytes 1671176 | tf_op jit(solution)/shard_map/ppermute | solution.py:163
  74.5 0.1 pad_add_fusion.where
  74.6 1.8 %collective-permute-done = bf16[4,4,136,128]{3,2,1,0:T(8,128)(2,1)S(1)} collective-permute-done((bf16[4,4,136,128]{3,2,1,0:T(8,128)(2,1)S(1)}, bf16[4,4,136,128]{3,2,1,0:T(8,128)(2,1)S(1)}, u32[]{:S(2)}, u32[]{:S(2)}) %collective-permute-start) | collective-permute-done | bytes 557088 | tf_op jit(solution)/shard_map/ppermute | solution.py:163
  76.4 0.1 select_bitcast_fusion.1
  76.5 0.1 pad_maximum_fusion
  76.6 0.0 copy-start
  76.6 9.3 %shard_map.51 = (f32[256,256]{1,0:T(8,128)S(1)}, f32[1,128]{1,0:T(1,128)}) custom-call(bf16[256,2048]{1,0:T(8,128)(2,1)S(1)} %bitcast.28, bf16[256,128]{1,0:T(8,128)(2,1)S(1)} %bitcast.30), custom_call_target="tpu_custom_call" | custom-call | flops 10000000000 | bytes 4000000 | tf_op jit(solution)/shard_map/pallas_call | solution.py:197
  86.0 10.2 %all-to-all-done.2.fac = bf16[16,256,128]{2,1,0:T(8,128)(2,1)S(1)} async-done(((bf16[16,256,128]{2,1,0:T(8,128)(2,1)}), bf16[16,256,128]{2,1,0:T(8,128)(2,1)S(1)}, u32[]{:S(2)}, u32[]{:S(2)}) %all-to-all-start.2) | async-done | bytes 1048608 | tf_op jit(solution)/shard_map/all_to_all | solution.py:194
  96.2 0.0 copy-done
  96.2 2.4 %shard_map.52 = f32[256,256]{1,0:T(8,128)} custom-call(s32[3]{0:T(128)S(1)} %pad_add_fusion.where, bf16[4096,128]{1,0:T(8,128)(2,1)S(1)} %copy-done, bf16[16,256,128]{2,1,0:T(8,128)(2,1)S(1)} %all-to-all-done.2.fac, bf16[256,128]{1,0:T(8,128)(2,1)S(1)} %bitcast.31, bf16[256,2048]{1,0:T(8,128)(2,1)S(1)} %bitcast.29, f32[256,256]{1,0:T(8,128)S(1)} %get-tuple-element.8.inverse), custom_call_target="tpu_custom_call" | custom-call | flops 1000000000 | bytes 4000000 | tf_op jit(solution)/shard_map/pallas_call | solution.py:212
  (4 shorter events, 0.0 us)
Async XLA Ops:
  2.8 15.1 %all-to-all-start = ((bf16[32,16,128]{2,1,0:T(8,128)(2,1)}), bf16[32,16,128]{2,1,0:T(8,128)(2,1)S(1)}, u32[]{:S(2)}, u32[]{:S(2)}) async-start(bf16[32,16,128]{2,1,0:T(8,128)(2,1)} %shard_map.50), calls=%async_computation | async-start | bytes 262144 | tf_op jit(solution)/shard_map/all_to_all | solution.py:151
  43.6 52.6 %all-to-all-start.2 = ((bf16[16,256,128]{2,1,0:T(8,128)(2,1)}), bf16[16,256,128]{2,1,0:T(8,128)(2,1)S(1)}, u32[]{:S(2)}, u32[]{:S(2)}) async-start(bf16[16,256,128]{2,1,0:T(8,128)(2,1)} %bitcast.2), calls=%async_computation.2 | async-start | bytes 2097152 | tf_op jit(solution)/shard_map/all_to_all | solution.py:194
  72.6 3.8 %collective-permute-start = (bf16[4,4,136,128]{3,2,1,0:T(8,128)(2,1)S(1)}, bf16[4,4,136,128]{3,2,1,0:T(8,128)(2,1)S(1)}, u32[]{:S(2)}, u32[]{:S(2)}) collective-permute-start(bf16[4,4,136,128]{3,2,1,0:T(8,128)(2,1)S(1)} %bitcast.32), channel_id=1, source_target_pairs={{0,16},{16,0},{32,48},{48,32},{64,80},{80,64},{96,112},{112,96},{1... | collective-permute-start | bytes 1671176 | tf_op jit(solution)/shard_map/ppermute | solution.py:163
  76.6 19.6 %copy-start = (bf16[4096,128]{1,0:T(8,128)(2,1)S(1)}, bf16[4096,128]{1,0:T(8,128)(2,1)}, u32[]{:S(2)}) copy-start(bf16[4096,128]{1,0:T(8,128)(2,1)} %feat.1) | copy-start | bytes 3145732

commit v4 on v3

--- a/solution.py
+++ b/solution.py
@@ -56,12 +56,17 @@
         inside = (lane_wide >= begin) & (lane_wide < begin + BLOCK)
         eye = lane_wide == begin + i * SUB + lax.broadcasted_iota(jnp.int32, (SUB, TILE), 0)
         rows.append(jnp.where(inside, eye.astype(jnp.float32), row))
-    for j in range(count):
+
+    def columns_of(j):
         first = begin - base + j * SUB
-        column = [
+        return [
             [jnp.broadcast_to(diag[i][:, first + k : first + k + 1], (SUB, LANES)) for k in range(SUB)]
             for i in range(j, count)
         ]
+
+    column = columns_of(0)
+    for j in range(count):
+        after = columns_of(j + 1) if j + 1 < count else []
         pivot = jnp.ones((SUB, LANES), jnp.float32)
         for k in range(SUB):
             value = jnp.broadcast_to(column[0][k][k : k + 1, :], (SUB, LANES))
@@ -73,6 +78,10 @@
                 other = jnp.broadcast_to(column[0][k][m : m + 1, :], (SUB, LANES))
                 for i in range(len(column)):
                     column[i][m] = column[i][m] - factor[i] * other
+            for m in range(SUB if after else 0):
+                other = jnp.broadcast_to(column[1][k][m : m + 1, :], (SUB, LANES))
+                for i in range(len(after)):
+                    after[i][m] = after[i][m] - factor[i + 1] * other
             row_k = jnp.broadcast_to(rows[j][k : k + 1, :], (SUB, TILE))
             diag_k = jnp.broadcast_to(diag[j][k : k + 1, :], (SUB, LANES))
             for i in range(len(column)):
@@ -81,6 +90,7 @@
         scale = 1.0 / jnp.sqrt(pivot)
         pivots = jnp.where(lane == block * count + j, pivot, pivots)
         rows[j] = rows[j] * jnp.concatenate([scale, scale], axis=1)
+        column = after
     whole = jnp.concatenate(rows, axis=0)
     inverse[begin : begin + BLOCK, :] = jnp.where(lane_wide < begin + BLOCK, whole, 0.0)
     return whole, pivots
@@ -112,24 +122,19 @@
     send[...] = jnp.concatenate([fac, feat], axis=1).astype(jnp.bfloat16)
 
 
-def diagonal_kernel(panel_fac, panel_feat, inverse, log_det, work):
+def factor_kernel(where, my_feat, panel_fac, panel_feat, inverse, log_det, kernel, work):
     row = lax.broadcasted_iota(jnp.int32, (TILE, TILE), 0)
     col = lax.broadcasted_iota(jnp.int32, (TILE, TILE), 1)
     feat = panel_feat[...]
     fac = panel_fac[...]
     work[...] = tile_kernel(feat, feat, row == col) - dot_last(fac, fac)
     log_det[...] = jnp.full((1, LANES), factor_tile(work, inverse), jnp.float32)
-
-
-def panel_kernel(where, feat, fac, panel_feat, panel_fac, inverse, panel):
-    tile_of = where[1]
-    panel_tile = where[2]
-    row = lax.broadcasted_iota(jnp.int32, (TILE, TILE), 0)
-    col = lax.broadcasted_iota(jnp.int32, (TILE, TILE), 1)
-    self_pair = (row == col) & (tile_of == panel_tile)
+    kernel[...] = tile_kernel(my_feat[...], feat, (row == col) & (where[1] == where[2]))
+
+
+def panel_kernel(where, fac, panel_fac, kernel, inverse, panel):
     rows = jnp.concatenate([fac[z] for z in range(fac.shape[0])], axis=1)
-    update = dot_last(rows, panel_fac[...])
-    block = tile_kernel(feat[...], panel_feat[...], self_pair) - update
+    block = kernel[...] - dot_last(rows, panel_fac[...])
     result = lax.dot_general(
         block,
         inverse[...],
@@ -137,7 +142,7 @@
         precision=lax.Precision.HIGHEST,
         preferred_element_type=jnp.float32,
     )
-    panel[...] = jnp.where(tile_of >= panel_tile, result, 0.0)
+    panel[...] = jnp.where(where[1] >= where[2], result, 0.0)
 
 
 def groups_of(axis):
@@ -193,40 +198,39 @@
     tiles, layers = lax.optimization_barrier((tiles, layers))
     my_fac = lax.all_to_all(tiles, "col", 0, 0, tiled=True)
     panel_fac, panel_feat = gather_chunks(layers, feat_rows)
-    vmem = pl.BlockSpec(memory_space=pltpu.VMEM)
-    inverse, log_det = pl.pallas_call(
-        diagonal_kernel,
+    tile_of = my_col * row_count + my_row
+    where = jnp.stack([my_col, tile_of, panel_tile]).astype(jnp.int32)
+    whole = lambda *shape: pl.BlockSpec(shape, lambda i, where: (0,) * len(shape))
+    inverse, log_det, kernel = pl.pallas_call(
+        factor_kernel,
         out_shape=(
             jax.ShapeDtypeStruct((TILE, TILE), jnp.float32),
             jax.ShapeDtypeStruct((1, LANES), jnp.float32),
+            jax.ShapeDtypeStruct((TILE, TILE), jnp.float32),
         ),
-        in_specs=[vmem, vmem],
-        out_specs=(vmem, vmem),
-        scratch_shapes=[pltpu.VMEM((TILE, TILE), jnp.float32)],
-        compiler_params=pltpu.CompilerParams(vmem_limit_bytes=VMEM_LIMIT),
-        cost_estimate=pl.CostEstimate(flops=10**10, bytes_accessed=4 * 10**6, transcendentals=10**5),
-    )(panel_fac, panel_feat)
-    tile_of = my_col * row_count + my_row
-    where = jnp.stack([my_col, tile_of, panel_tile]).astype(jnp.int32)
-    whole = lambda *shape: pl.BlockSpec(shape, lambda i, where: (0,) * len(shape))
-    panel = pl.pallas_call(
-        panel_kernel,
-        out_shape=jax.ShapeDtypeStruct((TILE, TILE), jnp.float32),
         grid_spec=pltpu.PrefetchScalarGridSpec(
             num_scalar_prefetch=1,
             grid=(1,),
             in_specs=[
                 pl.BlockSpec((TILE, FEAT), lambda i, where: (where[0], 0)),
-                whole(col_count, my_rows, width),
+                whole(TILE, col_count * width),
                 whole(TILE, FEAT),
-                whole(TILE, col_count * width),
-                whole(TILE, TILE),
             ],
-            out_specs=whole(TILE, TILE),
+            out_specs=(whole(TILE, TILE), whole(1, LANES), whole(TILE, TILE)),
+            scratch_shapes=[pltpu.VMEM((TILE, TILE), jnp.float32)],
         ),
         compiler_params=pltpu.CompilerParams(vmem_limit_bytes=VMEM_LIMIT),
+        cost_estimate=pl.CostEstimate(flops=10**10, bytes_accessed=4 * 10**6, transcendentals=10**5),
+    )(where, features, panel_fac, panel_feat)
+    vmem = pl.BlockSpec(memory_space=pltpu.VMEM)
+    panel = pl.pallas_call(
+        panel_kernel,
+        out_shape=jax.ShapeDtypeStruct((TILE, TILE), jnp.float32),
+        in_specs=[pl.BlockSpec(memory_space=pltpu.SMEM), vmem, vmem, vmem, vmem],
+        out_specs=vmem,
+        compiler_params=pltpu.CompilerParams(vmem_limit_bytes=VMEM_LIMIT),
         cost_estimate=pl.CostEstimate(flops=10**9, bytes_accessed=4 * 10**6, transcendentals=10**5),
-    )(where, features, my_fac, panel_feat, panel_fac, inverse)
+    )(where, my_fac, panel_fac, kernel, inverse)
     return (panel, log_det[0, :1])
 
 

time: 100 us -> 100 us (level)
  Pallas kernels: 13.3 us -> 12.1 us
  local copies, waits for them, and re-layouts: 0.02 us -> 1.12 us
    pallas_call x1, Pallas kernels: 9.33 us -> 8.14 us  [body(): pl.pallas_call(factor_kernel, out_shape=(jax.ShapeDtypeStruct((TILE, TILE...]
    unnamed x2, local copies, waits for them, and re-layouts: 0.01 us -> 1.11 us
  transfers between devices with their start and end apart: 3 -> 3, of which waited for: 3 -> 3; matrix products, arithmetic and copies ran while one was open for 0% -> 0% of each run, Pallas kernels for 9% -> 8%
where the time goes in v4:
time: 100 us; the launch traced here: 98.6 us
  blocking collectives  50.9 us (51%)
  waiting for transfers between devices  18 us (18%)
  starting transfers between devices  14.8 us (15%)
  Pallas kernels  12.1 us (12%)
  between operations  1.38 us (1%)
  local copies, waits for them, and re-layouts  1.12 us (1%)
    all_to_all x1, blocking collectives, gather_panel(): layers = lax.all_to_all(copies, 'col', 0, 0, tiled=True)  25.7 us
    all_gather x1, blocking collectives, gather_chunks(): lax.all_gather(over_x, 'row', axis=0, axis_index_groups=groups_of('y'))  13.2 us
    all_gather x1, blocking collectives, gather_chunks(): lax.all_gather(chunk, 'row', axis=0, axis_index_groups=groups_of('x'))  12 us
    all_to_all x1, waiting for transfers between devices, body(): my_fac = lax.all_to_all(tiles, 'col', 0, 0, tiled=True)  10.3 us
    all_to_all x1, starting transfers between devices, gather_panel(): got = lax.all_to_all(send, 'row', 0, 0, tiled=True)  9.27 us
    pallas_call x1, Pallas kernels, body(): pl.pallas_call(factor_kernel, out_shape=(jax.ShapeDtypeStruct((TILE, TILE...  8.14 us
    all_to_all x1, waiting for transfers between devices, gather_panel(): got = lax.all_to_all(send, 'row', 0, 0, tiled=True)  5.82 us
    all_to_all x1, starting transfers between devices, body(): my_fac = lax.all_to_all(tiles, 'col', 0, 0, tiled=True)  3.66 us
  transfers between devices with their start and end apart: 3, of which 3 were waited for; matrix products, arithmetic and copies ran while one was open for 0% of the time, Pallas kernels for 8%

profile of v4, /device:TPU:24, one launch (start us, length us, event | category | flops | bytes accessed | tf_op | source)
XLA Modules:
  0.0 98.6 jit_solution(12355895000654254407)
XLA Ops:
  1.3 1.6 %shard_map.50 = bf16[32,16,128]{2,1,0:T(8,128)(2,1)} custom-call(s32[1]{0:T(128)} %copy.7.panel_index, bf16[4096,128]{1,0:T(8,128)(2,1)} %my_feat.1, bf16[4096,128]{1,0:T(8,128)(2,1)} %factor_prev.1), custom_call_target="tpu_custom_call" | custom-call | tf_op jit(solution)/shard_map/pallas_call | solution.py:187
  2.8 9.3 %all-to-all-start = ((bf16[32,16,128]{2,1,0:T(8,128)(2,1)}), bf16[32,16,128]{2,1,0:T(8,128)(2,1)S(1)}, u32[]{:S(2)}, u32[]{:S(2)}) async-start(bf16[32,16,128]{2,1,0:T(8,128)(2,1)} %shard_map.50), calls=%async_computation | async-start | bytes 262144 | tf_op jit(solution)/shard_map/all_to_all | solution.py:156
  12.1 5.8 %all-to-all-done = bf16[32,16,128]{2,1,0:T(8,128)(2,1)S(1)} async-done(((bf16[32,16,128]{2,1,0:T(8,128)(2,1)}), bf16[32,16,128]{2,1,0:T(8,128)(2,1)S(1)}, u32[]{:S(2)}, u32[]{:S(2)}) %all-to-all-start) | async-done | bytes 131104 | tf_op jit(solution)/shard_map/all_to_all | solution.py:156
  18.0 25.7 %all_to_all.15 = bf16[16,8,128]{2,1,0:T(8,128)(2,1)S(1)} all-to-all(bf16[16,8,128]{2,1,0:T(8,128)(2,1)S(1)} %broadcast_in_dim.9), channel_id=1, replica_groups=mesh['row'=32,'col'=16] {'col'}, dimensions={0} | all-to-all | bytes 65536 | tf_op jit(solution)/shard_map/all_to_all | solution.py:159
  43.6 3.7 %all-to-all-start.2 = ((bf16[16,256,128]{2,1,0:T(8,128)(2,1)}), bf16[16,256,128]{2,1,0:T(8,128)(2,1)S(1)}, u32[]{:S(2)}, u32[]{:S(2)}) async-start(bf16[16,256,128]{2,1,0:T(8,128)(2,1)} %bitcast.2), calls=%async_computation.2 | async-start | bytes 2097152 | tf_op jit(solution)/shard_map/all_to_all | solution.py:199
  47.3 12.0 %all-gather = bf16[544,128]{1,0:T(8,128)(2,1)S(1)} all-gather(bf16[136,128]{1,0:T(8,128)(2,1)S(1)} %pad_maximum_fusion.1), channel_id=2, replica_groups={{0,32,64,96},{16,48,80,112},{128,160,192,224},{144,176,208,240},{256,28..., dimensions={0}, use_global_device_ids=true | all-gather | bytes 174080 | tf_op jit(solution)/shard_map/all_gather | solution.py:166
  59.3 13.2 %all-gather.1 = bf16[16,136,128]{2,1,0:T(8,128)(2,1)S(1)} all-gather(bf16[4,136,128]{2,1,0:T(8,128)(2,1)S(1)} %bitcast.33), channel_id=3, replica_groups={{0,128,256,384},{16,144,272,400},{32,160,288,416},{48,176,304,432},{64,..., dimensions={0}, use_global_device_ids=true | all-gather | bytes 696320 | tf_op jit(solution)/shard_map/all_gather | solution.py:167
  72.6 1.9 %collective-permute-start = (bf16[4,4,136,128]{3,2,1,0:T(8,128)(2,1)S(1)}, bf16[4,4,136,128]{3,2,1,0:T(8,128)(2,1)S(1)}, u32[]{:S(2)}, u32[]{:S(2)}) collective-permute-start(bf16[4,4,136,128]{3,2,1,0:T(8,128)(2,1)S(1)} %bitcast.31), channel_id=1, source_target_pairs={{0,16},{16,0},{32,48},{48,32},{64,80},{80,64},{96,112},{112,96},{1... | collective-permute-start | bytes 1671176 | tf_op jit(solution)/shard_map/ppermute | solution.py:168
  74.5 0.1 pad_add_fusion.where
  74.6 1.8 %collective-permute-done = bf16[4,4,136,128]{3,2,1,0:T(8,128)(2,1)S(1)} collective-permute-done((bf16[4,4,136,128]{3,2,1,0:T(8,128)(2,1)S(1)}, bf16[4,4,136,128]{3,2,1,0:T(8,128)(2,1)S(1)}, u32[]{:S(2)}, u32[]{:S(2)}) %collective-permute-start) | collective-permute-done | bytes 557088 | tf_op jit(solution)/shard_map/ppermute | solution.py:168
  76.4 0.1 select_bitcast_fusion
  76.5 0.0 copy-start
  76.5 0.1 fusion
  76.6 1.1 %copy-done = bf16[4096,128]{1,0:T(8,128)(2,1)S(1)} copy-done((bf16[4096,128]{1,0:T(8,128)(2,1)S(1)}, bf16[4096,128]{1,0:T(8,128)(2,1)}, u32[]{:S(2)}) %copy-start) | copy-done | bytes 1048600
  77.7 8.1 %shard_map.51 = (f32[256,256]{1,0:T(8,128)S(1)}, f32[1,128]{1,0:T(1,128)}, f32[256,256]{1,0:T(8,128)S(1)}) custom-call(s32[3]{0:T(128)S(1)} %pad_add_fusion.where, bf16[4096,128]{1,0:T(8,128)(2,1)S(1)} %copy-done, bf16[256,2048]{1,0:T(8,128)(2,1)S(1)} %bitcast.28, bf16[256,128]{1,0:T(8,128)(2,1)S(1)} %bitcast.30), custom_call_target="tpu_custom_call" | custom-call | flops 10000000000 | bytes 4000000 | tf_op jit(solution)/shard_map/pallas_call | solution.py:204
  85.9 10.3 %all-to-all-done.2.fac = bf16[16,256,128]{2,1,0:T(8,128)(2,1)S(1)} async-done(((bf16[16,256,128]{2,1,0:T(8,128)(2,1)}), bf16[16,256,128]{2,1,0:T(8,128)(2,1)S(1)}, u32[]{:S(2)}, u32[]{:S(2)}) %all-to-all-start.2) | async-done | bytes 1048608 | tf_op jit(solution)/shard_map/all_to_all | solution.py:199
  96.2 2.4 %shard_map.52 = f32[256,256]{1,0:T(8,128)} custom-call(s32[3]{0:T(128)S(1)} %pad_add_fusion.where, bf16[16,256,128]{2,1,0:T(8,128)(2,1)S(1)} %all-to-all-done.2.fac, bf16[256,2048]{1,0:T(8,128)(2,1)S(1)} %bitcast.29, f32[256,256]{1,0:T(8,128)S(1)} %get-tuple-element.9.kernel, f32[256,256]{1,0:T(8,128)S(1)} %get-tuple-element.10.inverse), custom_call_target="tpu_custom_call" | custom-call | flops 1000000000 | bytes 4000000 | tf_op jit(solution)/shard_map/pallas_call | solution.py:226
  (4 shorter events, 0.0 us)
Async XLA Ops:
  2.8 15.1 %all-to-all-start = ((bf16[32,16,128]{2,1,0:T(8,128)(2,1)}), bf16[32,16,128]{2,1,0:T(8,128)(2,1)S(1)}, u32[]{:S(2)}, u32[]{:S(2)}) async-start(bf16[32,16,128]{2,1,0:T(8,128)(2,1)} %shard_map.50), calls=%async_computation | async-start | bytes 262144 | tf_op jit(solution)/shard_map/all_to_all | solution.py:156
  43.6 52.6 %all-to-all-start.2 = ((bf16[16,256,128]{2,1,0:T(8,128)(2,1)}), bf16[16,256,128]{2,1,0:T(8,128)(2,1)S(1)}, u32[]{:S(2)}, u32[]{:S(2)}) async-start(bf16[16,256,128]{2,1,0:T(8,128)(2,1)} %bitcast.2), calls=%async_computation.2 | async-start | bytes 2097152 | tf_op jit(solution)/shard_map/all_to_all | solution.py:199
  72.6 3.8 %collective-permute-start = (bf16[4,4,136,128]{3,2,1,0:T(8,128)(2,1)S(1)}, bf16[4,4,136,128]{3,2,1,0:T(8,128)(2,1)S(1)}, u32[]{:S(2)}, u32[]{:S(2)}) collective-permute-start(bf16[4,4,136,128]{3,2,1,0:T(8,128)(2,1)S(1)} %bitcast.31), channel_id=1, source_target_pairs={{0,16},{16,0},{32,48},{48,32},{64,80},{80,64},{96,112},{112,96},{1... | collective-permute-start | bytes 1671176 | tf_op jit(solution)/shard_map/ppermute | solution.py:168
  76.5 1.2 %copy-start = (bf16[4096,128]{1,0:T(8,128)(2,1)S(1)}, bf16[4096,128]{1,0:T(8,128)(2,1)}, u32[]{:S(2)}) copy-start(bf16[4096,128]{1,0:T(8,128)(2,1)} %my_feat.1) | copy-start | bytes 3145732

commit v5 on v4

--- a/solution.py
+++ b/solution.py
@@ -10,7 +10,7 @@
 FEAT = 128
 NUGGET = 4.0
 RANGE = 8.0
-CHUNKS = 32
+CHUNKS = 8
 PIECE = TILE // CHUNKS
 BLOCK = 32
 SUB = 8
@@ -145,32 +145,35 @@
     panel[...] = jnp.where(where[1] >= where[2], result, 0.0)
 
 
-def groups_of(axis):
+def groups_of(*axes):
     index = np.arange(32).reshape(4, 4, 2)
-    return np.moveaxis(index, {"y": 0, "x": 1}[axis], 2).reshape(-1, 4).tolist()
+    place = [("y", "x", "core").index(axis) for axis in axes]
+    size = int(np.prod([index.shape[p] for p in place]))
+    return np.moveaxis(index, place, range(3 - len(place), 3)).reshape(-1, size).tolist()
 
 
 def gather_panel(send, owner_row):
     width = send.shape[2]
     col_count = lax.axis_size("col")
-    got = lax.all_to_all(send, "row", 0, 0, tiled=True)
-    slot = lax.dynamic_index_in_dim(got, owner_row, 0, keepdims=False)
+    got = lax.all_to_all(send, "row", 0, 0, tiled=True, axis_index_groups=groups_of("x", "core"))
+    slot = lax.dynamic_index_in_dim(got, owner_row % CHUNKS, 0, keepdims=False)
     copies = jnp.broadcast_to(slot[None, :PIECE], (col_count, PIECE, width))
     layers = lax.all_to_all(copies, "col", 0, 0, tiled=True)
     return layers, slot[PIECE:]
 
 
-def gather_chunks(layers, feat):
+def gather_chunks(layers, feat, owner_row):
     col_count, _, width = layers.shape
     chunk = jnp.concatenate([layers.reshape(col_count * PIECE, width), feat], axis=0)
-    over_x = lax.all_gather(chunk, "row", axis=0, axis_index_groups=groups_of("x"))
-    mine = lax.all_gather(over_x, "row", axis=0, axis_index_groups=groups_of("y"))
+    over_y = lax.all_gather(chunk, "row", axis=0, axis_index_groups=groups_of("y"))
+    chunk = lax.dynamic_index_in_dim(over_y, owner_row // CHUNKS, 0, keepdims=False)
+    mine = lax.all_gather(chunk, "row", axis=0, axis_index_groups=groups_of("x"))
     other = lax.ppermute(mine, "row", [(i, i ^ 1) for i in range(32)])
     first = lax.axis_index("row") % 2 == 0
-    both = jnp.stack([jnp.where(first, mine, other), jnp.where(first, other, mine)], axis=2)
-    fac = both[:, :, :, : col_count * PIECE].reshape(CHUNKS, col_count, PIECE, width)
+    both = jnp.stack([jnp.where(first, mine, other), jnp.where(first, other, mine)], axis=1)
+    fac = both[:, :, : col_count * PIECE].reshape(CHUNKS, col_count, PIECE, width)
     fac = fac.transpose(0, 2, 1, 3).reshape(TILE, col_count * width)
-    return fac, both[:, :, :, col_count * PIECE :].reshape(TILE, width)
+    return fac, both[:, :, col_count * PIECE :].reshape(TILE, width)
 
 
 def body(features, factor_prev, panel_index):
@@ -197,7 +200,7 @@
     layers, feat_rows = gather_panel(send, owner_row)
     tiles, layers = lax.optimization_barrier((tiles, layers))
     my_fac = lax.all_to_all(tiles, "col", 0, 0, tiled=True)
-    panel_fac, panel_feat = gather_chunks(layers, feat_rows)
+    panel_fac, panel_feat = gather_chunks(layers, feat_rows, owner_row)
     tile_of = my_col * row_count + my_row
     where = jnp.stack([my_col, tile_of, panel_tile]).astype(jnp.int32)
     whole = lambda *shape: pl.BlockSpec(shape, lambda i, where: (0,) * len(shape))

time: 100 us -> 98.5 us (0.985)
  starting transfers between devices: 14.8 us -> 10.1 us
  blocking collectives: 50.9 us -> 55.1 us
    all_to_all x1, starting transfers between devices: 9.27 us -> 4.3 us  [gather_panel(): lax.all_to_all(send, 'row', 0, 0, tiled=True, axis_index_groups=groups_of...]
    all_to_all x1, blocking collectives: 25.7 us -> 29.4 us  [gather_panel(): layers = lax.all_to_all(copies, 'col', 0, 0, tiled=True)]
    all_to_all x1, waiting for transfers between devices: 10.3 us -> 9.17 us  [body(): my_fac = lax.all_to_all(tiles, 'col', 0, 0, tiled=True)]
  transfers between devices with their start and end apart: 3 -> 3, of which waited for: 3 -> 3; matrix products, arithmetic and copies ran while one was open for 0% -> 1% of each run, Pallas kernels for 8% -> 8%
where the time goes in v5:
time: 98.5 us; the launch traced here: 98 us
  blocking collectives  55.1 us (56%)
  waiting for transfers between devices  17.1 us (17%)
  Pallas kernels  12.1 us (12%)
  starting transfers between devices  10.1 us (10%)
  local copies, waits for them, and re-layouts  1.93 us (2%)
  between operations  1.4 us (1%)
    all_to_all x1, blocking collectives, gather_panel(): layers = lax.all_to_all(copies, 'col', 0, 0, tiled=True)  29.4 us
    all_gather x1, blocking collectives, gather_chunks(): lax.all_gather(chunk, 'row', axis=0, axis_index_groups=groups_of('x'))  12.9 us
    all_gather x1, blocking collectives, gather_chunks(): lax.all_gather(chunk, 'row', axis=0, axis_index_groups=groups_of('y'))  12.8 us
    all_to_all x1, waiting for transfers between devices, body(): my_fac = lax.all_to_all(tiles, 'col', 0, 0, tiled=True)  9.17 us
    pallas_call x1, Pallas kernels, body(): pl.pallas_call(factor_kernel, out_shape=(jax.ShapeDtypeStruct((TILE, TILE...  8.14 us
    all_to_all x1, waiting for transfers between devices, gather_panel(): lax.all_to_all(send, 'row', 0, 0, tiled=True, axis_index_groups=groups_of...  6.14 us
    all_to_all x1, starting transfers between devices, gather_panel(): lax.all_to_all(send, 'row', 0, 0, tiled=True, axis_index_groups=groups_of...  4.3 us
    all_to_all x1, starting transfers between devices, body(): my_fac = lax.all_to_all(tiles, 'col', 0, 0, tiled=True)  3.9 us
  transfers between devices with their start and end apart: 3, of which 3 were waited for; matrix products, arithmetic and copies ran while one was open for 1% of the time, Pallas kernels for 8%

profile of v5, /device:TPU:24, one launch (start us, length us, event | category | flops | bytes accessed | tf_op | source)
XLA Modules:
  0.0 98.0 jit_solution(13799245609057825130)
XLA Ops:
  1.3 1.6 %shard_map.50 = bf16[8,64,128]{2,1,0:T(8,128)(2,1)} custom-call(s32[1]{0:T(128)} %copy.13.panel_index, bf16[4096,128]{1,0:T(8,128)(2,1)} %my_feat.1, bf16[4096,128]{1,0:T(8,128)(2,1)} %factor_prev.1), custom_call_target="tpu_custom_call" | custom-call | tf_op jit(solution)/shard_map/pallas_call | solution.py:190
  2.8 4.3 %all-to-all-start = ((bf16[8,64,128]{2,1,0:T(8,128)(2,1)}), bf16[8,64,128]{2,1,0:T(8,128)(2,1)S(1)}, u32[]{:S(2)}, u32[]{:S(2)}) async-start(bf16[8,64,128]{2,1,0:T(8,128)(2,1)} %shard_map.50), calls=%async_computation | async-start | bytes 262144 | tf_op jit(solution)/shard_map/all_to_all | solution.py:158
  7.1 6.1 %all-to-all-done = bf16[8,64,128]{2,1,0:T(8,128)(2,1)S(1)} async-done(((bf16[8,64,128]{2,1,0:T(8,128)(2,1)}), bf16[8,64,128]{2,1,0:T(8,128)(2,1)S(1)}, u32[]{:S(2)}, u32[]{:S(2)}) %all-to-all-start) | async-done | bytes 131104 | tf_op jit(solution)/shard_map/all_to_all | solution.py:158
  13.3 29.4 %all_to_all.15 = bf16[16,32,128]{2,1,0:T(8,128)(2,1)S(1)} all-to-all(bf16[16,32,128]{2,1,0:T(8,128)(2,1)S(1)} %broadcast_in_dim.9), channel_id=1, replica_groups=mesh['row'=32,'col'=16] {'col'}, dimensions={0} | all-to-all | bytes 262144 | tf_op jit(solution)/shard_map/all_to_all | solution.py:161
  42.7 3.9 %all-to-all-start.2 = ((bf16[16,256,128]{2,1,0:T(8,128)(2,1)}), bf16[16,256,128]{2,1,0:T(8,128)(2,1)S(1)}, u32[]{:S(2)}, u32[]{:S(2)}) async-start(bf16[16,256,128]{2,1,0:T(8,128)(2,1)} %bitcast.2), calls=%async_computation.2 | async-start | bytes 2097152 | tf_op jit(solution)/shard_map/all_to_all | solution.py:202
  46.7 12.8 %all-gather = bf16[2176,128]{1,0:T(8,128)(2,1)S(1)} all-gather(bf16[544,128]{1,0:T(8,128)(2,1)S(1)} %pad_maximum_fusion), channel_id=2, replica_groups={{0,128,256,384},{16,144,272,400},{32,160,288,416},{48,176,304,432},{64,..., dimensions={0}, use_global_device_ids=true | all-gather | bytes 696320 | tf_op jit(solution)/shard_map/all_gather | solution.py:168
  59.6 12.9 %all_gather.12 = bf16[4,544,128]{2,1,0:T(8,128)(2,1)S(1)} all-gather(bf16[1,544,128]{2,1,0:T(8,128)(2,1)S(1)} %constant_dynamic-slice_fusion), channel_id=1, replica_groups={{0,32,64,96},{16,48,80,112},{128,160,192,224},{144,176,208,240},{256,28..., dimensions={0}, use_global_device_ids=true | all-gather | bytes 696320 | tf_op jit(solution)/shard_map/all_gather | solution.py:170
  72.4 1.9 %collective-permute-start = (bf16[4,544,128]{2,1,0:T(8,128)(2,1)S(1)}, bf16[4,544,128]{2,1,0:T(8,128)(2,1)S(1)}, u32[]{:S(2)}, u32[]{:S(2)}) collective-permute-start(bf16[4,544,128]{2,1,0:T(8,128)(2,1)S(1)} %all_gather.12), channel_id=1, source_target_pairs={{0,16},{16,0},{32,48},{48,32},{64,80},{80,64},{96,112},{112,96},{1... | collective-permute-start | bytes 1671176 | tf_op jit(solution)/shard_map/ppermute | solution.py:171
  74.3 0.1 pad_add_fusion.where
  74.4 1.8 %collective-permute-done = bf16[4,544,128]{2,1,0:T(8,128)(2,1)S(1)} collective-permute-done((bf16[4,544,128]{2,1,0:T(8,128)(2,1)S(1)}, bf16[4,544,128]{2,1,0:T(8,128)(2,1)S(1)}, u32[]{:S(2)}, u32[]{:S(2)}) %collective-permute-start) | collective-permute-done | bytes 557088 | tf_op jit(solution)/shard_map/ppermute | solution.py:171
  76.2 0.1 select_bitcast_fusion
  76.3 0.1 fusion
  76.4 0.4 copy.9
  76.9 0.3 copy.12
  77.1 0.0 copy-start
  77.2 1.2 %copy-done = bf16[4096,128]{1,0:T(8,128)(2,1)S(1)} copy-done((bf16[4096,128]{1,0:T(8,128)(2,1)S(1)}, bf16[4096,128]{1,0:T(8,128)(2,1)}, u32[]{:S(2)}) %copy-start) | copy-done | bytes 1048600
  78.4 8.1 %shard_map.51 = (f32[256,256]{1,0:T(8,128)S(1)}, f32[1,128]{1,0:T(1,128)}, f32[256,256]{1,0:T(8,128)S(1)}) custom-call(s32[3]{0:T(128)S(1)} %pad_add_fusion.where, bf16[4096,128]{1,0:T(8,128)(2,1)S(1)} %copy-done, bf16[256,2048]{1,0:T(8,128)(2,1)S(1)} %bitcast.30, bf16[256,128]{1,0:T(8,128)(2,1)S(1)} %bitcast.32), custom_call_target="tpu_custom_call" | custom-call | flops 10000000000 | bytes 4000000 | tf_op jit(solution)/shard_map/pallas_call | solution.py:207
  86.5 9.2 %all-to-all-done.2.fac = bf16[16,256,128]{2,1,0:T(8,128)(2,1)S(1)} async-done(((bf16[16,256,128]{2,1,0:T(8,128)(2,1)}), bf16[16,256,128]{2,1,0:T(8,128)(2,1)S(1)}, u32[]{:S(2)}, u32[]{:S(2)}) %all-to-all-start.2) | async-done | bytes 1048608 | tf_op jit(solution)/shard_map/all_to_all | solution.py:202
  95.7 2.4 %shard_map.52 = f32[256,256]{1,0:T(8,128)} custom-call(s32[3]{0:T(128)S(1)} %pad_add_fusion.where, bf16[16,256,128]{2,1,0:T(8,128)(2,1)S(1)} %all-to-all-done.2.fac, bf16[256,2048]{1,0:T(8,128)(2,1)S(1)} %bitcast.31, f32[256,256]{1,0:T(8,128)S(1)} %get-tuple-element.9.kernel, f32[256,256]{1,0:T(8,128)S(1)} %get-tuple-element.10.inverse), custom_call_target="tpu_custom_call" | custom-call | flops 1000000000 | bytes 4000000 | tf_op jit(solution)/shard_map/pallas_call | solution.py:229
  (5 shorter events, 0.1 us)
Async XLA Ops:
  2.8 10.4 %all-to-all-start = ((bf16[8,64,128]{2,1,0:T(8,128)(2,1)}), bf16[8,64,128]{2,1,0:T(8,128)(2,1)S(1)}, u32[]{:S(2)}, u32[]{:S(2)}) async-start(bf16[8,64,128]{2,1,0:T(8,128)(2,1)} %shard_map.50), calls=%async_computation | async-start | bytes 262144 | tf_op jit(solution)/shard_map/all_to_all | solution.py:158
  42.7 52.9 %all-to-all-start.2 = ((bf16[16,256,128]{2,1,0:T(8,128)(2,1)}), bf16[16,256,128]{2,1,0:T(8,128)(2,1)S(1)}, u32[]{:S(2)}, u32[]{:S(2)}) async-start(bf16[16,256,128]{2,1,0:T(8,128)(2,1)} %bitcast.2), calls=%async_computation.2 | async-start | bytes 2097152 | tf_op jit(solution)/shard_map/all_to_all | solution.py:202
  72.4 3.8 %collective-permute-start = (bf16[4,544,128]{2,1,0:T(8,128)(2,1)S(1)}, bf16[4,544,128]{2,1,0:T(8,128)(2,1)S(1)}, u32[]{:S(2)}, u32[]{:S(2)}) collective-permute-start(bf16[4,544,128]{2,1,0:T(8,128)(2,1)S(1)} %all_gather.12), channel_id=1, source_target_pairs={{0,16},{16,0},{32,48},{48,32},{64,80},{80,64},{96,112},{112,96},{1... | collective-permute-start | bytes 1671176 | tf_op jit(solution)/shard_map/ppermute | solution.py:171
  77.1 1.2 %copy-start = (bf16[4096,128]{1,0:T(8,128)(2,1)S(1)}, bf16[4096,128]{1,0:T(8,128)(2,1)}, u32[]{:S(2)}) copy-start(bf16[4096,128]{1,0:T(8,128)(2,1)} %my_feat.1) | copy-start | bytes 3145732

commit v6 on v5

--- a/solution.py
+++ b/solution.py
@@ -15,7 +15,7 @@
 BLOCK = 32
 SUB = 8
 LANES = 128
-VMEM_LIMIT = 40 * 2**20
+VMEM_LIMIT = 16 * 2**20
 
 
 def tile_kernel(row_feat, panel_feat, self_pair):
@@ -116,25 +116,25 @@
     return jnp.sum(jnp.log(pivots)) / TILE
 
 
-def send_kernel(panel_index, features, factor_prev, send):
-    fac = factor_prev[...].astype(jnp.float32).reshape(CHUNKS, PIECE, LANES)
-    feat = features[...].astype(jnp.float32).reshape(CHUNKS, PIECE, LANES)
-    send[...] = jnp.concatenate([fac, feat], axis=1).astype(jnp.bfloat16)
-
-
-def factor_kernel(where, my_feat, panel_fac, panel_feat, inverse, log_det, kernel, work):
+def send_kernel(panel_index, factor_prev, send):
+    send[...] = factor_prev[...].reshape(CHUNKS, PIECE, LANES)
+
+
+def factor_kernel(panel_fac, panel_feat, inverse, log_det, work):
     row = lax.broadcasted_iota(jnp.int32, (TILE, TILE), 0)
     col = lax.broadcasted_iota(jnp.int32, (TILE, TILE), 1)
     feat = panel_feat[...]
     fac = panel_fac[...]
     work[...] = tile_kernel(feat, feat, row == col) - dot_last(fac, fac)
     log_det[...] = jnp.full((1, LANES), factor_tile(work, inverse), jnp.float32)
-    kernel[...] = tile_kernel(my_feat[...], feat, (row == col) & (where[1] == where[2]))
-
-
-def panel_kernel(where, fac, panel_fac, kernel, inverse, panel):
+
+
+def panel_kernel(where, fac, panel_fac, feat, panel_feat, inverse, panel):
+    row = lax.broadcasted_iota(jnp.int32, (TILE, TILE), 0)
+    col = lax.broadcasted_iota(jnp.int32, (TILE, TILE), 1)
+    kernel = tile_kernel(feat[...], panel_feat[...], (row == col) & (where[0] == where[1]))
     rows = jnp.concatenate([fac[z] for z in range(fac.shape[0])], axis=1)
-    block = kernel[...] - dot_last(rows, panel_fac[...])
+    block = kernel - dot_last(rows, panel_fac[...])
     result = lax.dot_general(
         block,
         inverse[...],
@@ -142,7 +142,7 @@
         precision=lax.Precision.HIGHEST,
         preferred_element_type=jnp.float32,
     )
-    panel[...] = jnp.where(where[1] >= where[2], result, 0.0)
+    panel[...] = jnp.where(where[0] >= where[1], result, 0.0)
 
 
 def groups_of(*axes):
@@ -156,24 +156,25 @@
     width = send.shape[2]
     col_count = lax.axis_size("col")
     got = lax.all_to_all(send, "row", 0, 0, tiled=True, axis_index_groups=groups_of("x", "core"))
-    slot = lax.dynamic_index_in_dim(got, owner_row % CHUNKS, 0, keepdims=False)
-    copies = jnp.broadcast_to(slot[None, :PIECE], (col_count, PIECE, width))
-    layers = lax.all_to_all(copies, "col", 0, 0, tiled=True)
-    return layers, slot[PIECE:]
-
-
-def gather_chunks(layers, feat, owner_row):
+    slot = lax.dynamic_index_in_dim(got, owner_row % CHUNKS, 0, keepdims=True)
+    copies = jnp.broadcast_to(slot, (col_count, PIECE, width))
+    return lax.all_to_all(copies, "col", 0, 0, tiled=True)
+
+
+def gather_chunks(layers, own_feat, owner_row):
     col_count, _, width = layers.shape
-    chunk = jnp.concatenate([layers.reshape(col_count * PIECE, width), feat], axis=0)
+    rows = col_count * PIECE
+    chunk = jnp.concatenate([layers.reshape(rows, width), own_feat], axis=0)
     over_y = lax.all_gather(chunk, "row", axis=0, axis_index_groups=groups_of("y"))
     chunk = lax.dynamic_index_in_dim(over_y, owner_row // CHUNKS, 0, keepdims=False)
     mine = lax.all_gather(chunk, "row", axis=0, axis_index_groups=groups_of("x"))
     other = lax.ppermute(mine, "row", [(i, i ^ 1) for i in range(32)])
     first = lax.axis_index("row") % 2 == 0
     both = jnp.stack([jnp.where(first, mine, other), jnp.where(first, other, mine)], axis=1)
-    fac = both[:, :, : col_count * PIECE].reshape(CHUNKS, col_count, PIECE, width)
+    both = both.reshape(CHUNKS, rows + TILE, width)
+    fac = both[:, :rows].reshape(CHUNKS, col_count, PIECE, width)
     fac = fac.transpose(0, 2, 1, 3).reshape(TILE, col_count * width)
-    return fac, both[:, :, col_count * PIECE :].reshape(TILE, width)
+    return fac, lax.dynamic_index_in_dim(both, owner_row % CHUNKS, 0, keepdims=False)[rows:]
 
 
 def body(features, factor_prev, panel_index):
@@ -186,54 +187,45 @@
     my_col = lax.axis_index("col")
     my_row = lax.axis_index("row")
     tiles = factor_prev.reshape(col_count, my_rows, width)
-    tile_rows = pl.BlockSpec((TILE, LANES), lambda i, index: (lax.div(index[0], row_count), 0))
     send = pl.pallas_call(
         send_kernel,
-        out_shape=jax.ShapeDtypeStruct((CHUNKS, 2 * PIECE, LANES), jnp.bfloat16),
+        out_shape=jax.ShapeDtypeStruct((CHUNKS, PIECE, LANES), jnp.bfloat16),
         grid_spec=pltpu.PrefetchScalarGridSpec(
             num_scalar_prefetch=1,
             grid=(1,),
-            in_specs=[tile_rows, tile_rows],
-            out_specs=pl.BlockSpec((CHUNKS, 2 * PIECE, LANES), lambda i, index: (0, 0, 0)),
+            in_specs=[pl.BlockSpec((TILE, LANES), lambda i, index: (lax.div(index[0], row_count), 0))],
+            out_specs=pl.BlockSpec((CHUNKS, PIECE, LANES), lambda i, index: (0, 0, 0)),
         ),
-    )(panel_index, features, factor_prev)
-    layers, feat_rows = gather_panel(send, owner_row)
-    tiles, layers = lax.optimization_barrier((tiles, layers))
+    )(panel_index, factor_prev)
+    layers = gather_panel(send, owner_row)
+    tiles, features, layers = lax.optimization_barrier((tiles, features, layers))
     my_fac = lax.all_to_all(tiles, "col", 0, 0, tiled=True)
-    panel_fac, panel_feat = gather_chunks(layers, feat_rows, owner_row)
-    tile_of = my_col * row_count + my_row
-    where = jnp.stack([my_col, tile_of, panel_tile]).astype(jnp.int32)
-    whole = lambda *shape: pl.BlockSpec(shape, lambda i, where: (0,) * len(shape))
-    inverse, log_det, kernel = pl.pallas_call(
+    own_feat = lax.dynamic_slice_in_dim(features, panel_tile // row_count * TILE, TILE, 0)
+    panel_fac, panel_feat = gather_chunks(layers, own_feat, owner_row)
+    my_feat = lax.dynamic_slice_in_dim(features, my_col * my_rows, my_rows, 0)
+    vmem = pl.BlockSpec(memory_space=pltpu.VMEM)
+    inverse, log_det = pl.pallas_call(
         factor_kernel,
         out_shape=(
             jax.ShapeDtypeStruct((TILE, TILE), jnp.float32),
             jax.ShapeDtypeStruct((1, LANES), jnp.float32),
-            jax.ShapeDtypeStruct((TILE, TILE), jnp.float32),
         ),
-        grid_spec=pltpu.PrefetchScalarGridSpec(
-            num_scalar_prefetch=1,
-            grid=(1,),
-            in_specs=[
-                pl.BlockSpec((TILE, FEAT), lambda i, where: (where[0], 0)),
-                whole(TILE, col_count * width),
-                whole(TILE, FEAT),
-            ],
-            out_specs=(whole(TILE, TILE), whole(1, LANES), whole(TILE, TILE)),
-            scratch_shapes=[pltpu.VMEM((TILE, TILE), jnp.float32)],
-        ),
+        in_specs=[vmem, vmem],
+        out_specs=(vmem, vmem),
+        scratch_shapes=[pltpu.VMEM((TILE, TILE), jnp.float32)],
         compiler_params=pltpu.CompilerParams(vmem_limit_bytes=VMEM_LIMIT),
-        cost_estimate=pl.CostEstimate(flops=10**10, bytes_accessed=4 * 10**6, transcendentals=10**5),
-    )(where, features, panel_fac, panel_feat)
-    vmem = pl.BlockSpec(memory_space=pltpu.VMEM)
+        cost_estimate=pl.CostEstimate(flops=8 * 10**9, bytes_accessed=4 * 10**6, transcendentals=10**5),
+    )(panel_fac, panel_feat)
+    tile_of = my_col * row_count + my_row
+    where = jnp.stack([tile_of, panel_tile]).astype(jnp.int32)
     panel = pl.pallas_call(
         panel_kernel,
         out_shape=jax.ShapeDtypeStruct((TILE, TILE), jnp.float32),
-        in_specs=[pl.BlockSpec(memory_space=pltpu.SMEM), vmem, vmem, vmem, vmem],
+        in_specs=[pl.BlockSpec(memory_space=pltpu.SMEM), vmem, vmem, vmem, vmem, vmem],
         out_specs=vmem,
         compiler_params=pltpu.CompilerParams(vmem_limit_bytes=VMEM_LIMIT),
         cost_estimate=pl.CostEstimate(flops=10**9, bytes_accessed=4 * 10**6, transcendentals=10**5),
-    )(where, my_fac, panel_fac, kernel, inverse)
+    )(where, my_fac, panel_fac, my_feat, panel_feat, inverse)
     return (panel, log_det[0, :1])
 
 

time: 98.5 us -> 98.3 us (level)
  blocking collectives: 55.1 us -> 57.1 us
  waiting for transfers between devices: 17.1 us -> 15.7 us
    all_to_all x1, waiting for transfers between devices: 9.17 us -> 7.9 us  [body(): my_fac = lax.all_to_all(tiles, 'col', 0, 0, tiled=True)]
    unnamed x3 -> x1, local copies, waits for them, and re-layouts: 1.48 us -> 0.27 us
    all_gather x1, blocking collectives: 12.8 us -> 14 us  [gather_chunks(): lax.all_gather(chunk, 'row', axis=0, axis_index_groups=groups_of('y'))]
  transfers between devices with their start and end apart: 3 -> 3, of which waited for: 3 -> 3; matrix products, arithmetic and copies ran while one was open for 1% -> 2% of each run, Pallas kernels for 8% -> 8%
where the time goes in v6:
time: 98.3 us; the launch traced here: 97.8 us
  blocking collectives  57.1 us (58%)
  waiting for transfers between devices  15.7 us (16%)
  Pallas kernels  11.4 us (12%)
  starting transfers between devices  9.96 us (10%)
  local copies, waits for them, and re-layouts  1.8 us (2%)
  between operations  1.44 us (1%)
    all_to_all x1, blocking collectives, gather_panel(): return lax.all_to_all(copies, 'col', 0, 0, tiled=True)  29.7 us
    all_gather x1, blocking collectives, gather_chunks(): lax.all_gather(chunk, 'row', axis=0, axis_index_groups=groups_of('y'))  14 us
    all_gather x1, blocking collectives, gather_chunks(): lax.all_gather(chunk, 'row', axis=0, axis_index_groups=groups_of('x'))  13.4 us
    all_to_all x1, waiting for transfers between devices, body(): my_fac = lax.all_to_all(tiles, 'col', 0, 0, tiled=True)  7.9 us
    pallas_call x1, Pallas kernels, body(): pl.pallas_call(factor_kernel, out_shape=(jax.ShapeDtypeStruct((TILE, TILE...  7.5 us
    all_to_all x1, waiting for transfers between devices, gather_panel(): lax.all_to_all(send, 'row', 0, 0, tiled=True, axis_index_groups=groups_of...  5.62 us
    all_to_all x1, starting transfers between devices, gather_panel(): lax.all_to_all(send, 'row', 0, 0, tiled=True, axis_index_groups=groups_of...  4.3 us
    all_to_all x1, starting transfers between devices, body(): my_fac = lax.all_to_all(tiles, 'col', 0, 0, tiled=True)  3.75 us
  transfers between devices with their start and end apart: 3, of which 3 were waited for; matrix products, arithmetic and copies ran while one was open for 2% of the time, Pallas kernels for 8%

profile of v6, /device:TPU:24, one launch (start us, length us, event | category | flops | bytes accessed | tf_op | source)
XLA Modules:
  0.0 97.8 jit_solution(16646939175529306949)
XLA Ops:
  1.3 1.5 %shard_map.50 = bf16[8,32,128]{2,1,0:T(8,128)(2,1)} custom-call(s32[1]{0:T(128)} %copy.12.panel_index, bf16[4096,128]{1,0:T(8,128)(2,1)} %factor_prev.1), custom_call_target="tpu_custom_call" | custom-call | tf_op jit(solution)/shard_map/pallas_call | solution.py:190
  2.8 4.3 %all-to-all-start = ((bf16[8,32,128]{2,1,0:T(8,128)(2,1)}), bf16[8,32,128]{2,1,0:T(8,128)(2,1)S(1)}, u32[]{:S(2)}, u32[]{:S(2)}) async-start(bf16[8,32,128]{2,1,0:T(8,128)(2,1)} %shard_map.50), calls=%async_computation | async-start | bytes 131072 | tf_op jit(solution)/shard_map/all_to_all | solution.py:158
  7.1 5.6 %all-to-all-done = bf16[8,32,128]{2,1,0:T(8,128)(2,1)S(1)} async-done(((bf16[8,32,128]{2,1,0:T(8,128)(2,1)}), bf16[8,32,128]{2,1,0:T(8,128)(2,1)S(1)}, u32[]{:S(2)}, u32[]{:S(2)}) %all-to-all-start) | async-done | bytes 65568 | tf_op jit(solution)/shard_map/all_to_all | solution.py:158
  12.7 29.7 %all_to_all.15 = bf16[16,32,128]{2,1,0:T(8,128)(2,1)S(1)} all-to-all(bf16[16,32,128]{2,1,0:T(8,128)(2,1)S(1)} %broadcast_in_dim.8), channel_id=1, replica_groups=mesh['row'=32,'col'=16] {'col'}, dimensions={0} | all-to-all | bytes 262144 | tf_op jit(solution)/shard_map/all_to_all | solution.py:161
  42.4 3.7 %all-to-all-start.2 = ((bf16[16,256,128]{2,1,0:T(8,128)(2,1)}), bf16[16,256,128]{2,1,0:T(8,128)(2,1)S(1)}, u32[]{:S(2)}, u32[]{:S(2)}) async-start(bf16[16,256,128]{2,1,0:T(8,128)(2,1)} %bitcast.1), calls=%async_computation.2 | async-start | bytes 2097152 | tf_op jit(solution)/shard_map/all_to_all | solution.py:202
  46.2 0.9 constant_dynamic-slice_fusion
  47.1 14.0 %all-gather = bf16[3072,128]{1,0:T(8,128)(2,1)S(1)} all-gather(bf16[768,128]{1,0:T(8,128)(2,1)S(1)} %pad_maximum_fusion.1), channel_id=2, replica_groups={{0,128,256,384},{16,144,272,400},{32,160,288,416},{48,176,304,432},{64,..., dimensions={0}, use_global_device_ids=true | all-gather | bytes 983040 | tf_op jit(solution)/shard_map/all_gather | solution.py:168
  61.1 13.4 %all_gather.12 = bf16[4,768,128]{2,1,0:T(8,128)(2,1)S(1)} all-gather(bf16[1,768,128]{2,1,0:T(8,128)(2,1)S(1)} %constant_dynamic-slice_fusion.1), channel_id=1, replica_groups={{0,32,64,96},{16,48,80,112},{128,160,192,224},{144,176,208,240},{256,28..., dimensions={0}, use_global_device_ids=true | all-gather | bytes 983040 | tf_op jit(solution)/shard_map/all_gather | solution.py:170
  74.5 1.9 %collective-permute-start = (bf16[4,768,128]{2,1,0:T(8,128)(2,1)S(1)}, bf16[4,768,128]{2,1,0:T(8,128)(2,1)S(1)}, u32[]{:S(2)}, u32[]{:S(2)}) collective-permute-start(bf16[4,768,128]{2,1,0:T(8,128)(2,1)S(1)} %all_gather.12), channel_id=1, source_target_pairs={{0,16},{16,0},{32,48},{48,32},{64,80},{80,64},{96,112},{112,96},{1... | collective-permute-start | bytes 2359304 | tf_op jit(solution)/shard_map/ppermute | solution.py:171
  76.5 0.1 pad_add_fusion.where
  76.5 2.2 %collective-permute-done = bf16[4,768,128]{2,1,0:T(8,128)(2,1)S(1)} collective-permute-done((bf16[4,768,128]{2,1,0:T(8,128)(2,1)S(1)}, bf16[4,768,128]{2,1,0:T(8,128)(2,1)S(1)}, u32[]{:S(2)}, u32[]{:S(2)}) %collective-permute-start) | collective-permute-done | bytes 786464 | tf_op jit(solution)/shard_map/ppermute | solution.py:171
  78.7 0.2 select_bitcast_fusion.1
  78.9 0.1 pad_maximum_fusion
  79.1 0.1 copy.7
  79.2 0.1 slice.16
  79.3 0.4 copy.8
  79.7 0.3 copy.11
  80.0 7.5 %shard_map.51 = (f32[256,256]{1,0:T(8,128)S(1)}, f32[1,128]{1,0:T(1,128)}) custom-call(bf16[256,2048]{1,0:T(8,128)(2,1)S(1)} %bitcast.28, bf16[256,128]{1,0:T(8,128)(2,1)S(1)} %dynamic-slice_bitcast_fusion.panel_feat), custom_call_target="tpu_custom_call" | custom-call | flops 8000000000 | bytes 4000000 | tf_op jit(solution)/shard_map/pallas_call | solution.py:207
  87.5 7.9 %all-to-all-done.2.fac = bf16[16,256,128]{2,1,0:T(8,128)(2,1)S(1)} async-done(((bf16[16,256,128]{2,1,0:T(8,128)(2,1)}), bf16[16,256,128]{2,1,0:T(8,128)(2,1)S(1)}, u32[]{:S(2)}, u32[]{:S(2)}) %all-to-all-start.2) | async-done | bytes 1048608 | tf_op jit(solution)/shard_map/all_to_all | solution.py:202
  95.4 2.4 %shard_map.52 = f32[256,256]{1,0:T(8,128)} custom-call(s32[2]{0:T(128)S(1)} %pad_add_fusion.where, bf16[16,256,128]{2,1,0:T(8,128)(2,1)S(1)} %all-to-all-done.2.fac, bf16[256,2048]{1,0:T(8,128)(2,1)S(1)} %bitcast.29, bf16[256,128]{1,0:T(8,128)(2,1)S(1)} %get-tuple-element.14.feat, bf16[256,128]{1,0:T(8,128)(2,1)S(1)} %dynamic-slice_bitcast_fusion.panel_feat, ...), custom_call_target="tpu_custom_call" | custom-call | flops 1000000000 | bytes 4000000 | tf_op jit(solution)/shard_map/pallas_call | solution.py:221
  (5 shorter events, 0.1 us)
Async XLA Ops:
  2.8 9.9 %all-to-all-start = ((bf16[8,32,128]{2,1,0:T(8,128)(2,1)}), bf16[8,32,128]{2,1,0:T(8,128)(2,1)S(1)}, u32[]{:S(2)}, u32[]{:S(2)}) async-start(bf16[8,32,128]{2,1,0:T(8,128)(2,1)} %shard_map.50), calls=%async_computation | async-start | bytes 131072 | tf_op jit(solution)/shard_map/all_to_all | solution.py:158
  42.4 53.0 %all-to-all-start.2 = ((bf16[16,256,128]{2,1,0:T(8,128)(2,1)}), bf16[16,256,128]{2,1,0:T(8,128)(2,1)S(1)}, u32[]{:S(2)}, u32[]{:S(2)}) async-start(bf16[16,256,128]{2,1,0:T(8,128)(2,1)} %bitcast.1), calls=%async_computation.2 | async-start | bytes 2097152 | tf_op jit(solution)/shard_map/all_to_all | solution.py:202
  74.5 4.2 %collective-permute-start = (bf16[4,768,128]{2,1,0:T(8,128)(2,1)S(1)}, bf16[4,768,128]{2,1,0:T(8,128)(2,1)S(1)}, u32[]{:S(2)}, u32[]{:S(2)}) collective-permute-start(bf16[4,768,128]{2,1,0:T(8,128)(2,1)S(1)} %all_gather.12), channel_id=1, source_target_pairs={{0,16},{16,0},{32,48},{48,32},{64,80},{80,64},{96,112},{112,96},{1... | collective-permute-start | bytes 2359304 | tf_op jit(solution)/shard_map/ppermute | solution.py:171
